TPU v7x, 32 devices: a whole 2x2x4 slice. The times are simulated.
32 devices in a mesh: parts: 2 (over y), group: 4 (over z), tile: 4 (over x, core).
Axes of the slice: x: 2, y: 2, z: 4, core: 2. Of those that a mesh axis runs over, the one named last changes fastest.
Arguments:
- product_codes: int32 [12288, 96], P(('parts', 'group', 'tile')), parts along dimension 0, may hold values from 0 to 255
- member_cluster: int32 [12288], P(('parts', 'group', 'tile')), parts along dimension 0, may hold values from 0 to 6143, as said below
- member_slot: int32 [12288], P(('parts', 'group', 'tile')), parts along dimension 0, may hold values from 0 to 12287, as said below
- codebook: bfloat16 [256, 768], replicated, may hold values from -14 to 14
Outputs:
- best_cosine: float32 [12288], P(('parts', 'group', 'tile')), parts along dimension 0
There are 2 independent parts, one for each index of `parts`. A program takes and returns all parts, laid end to end along the dimension named above; an argument that names none is the same for every part. Nothing has to cross between parts.
Inputs may be any that keep to these rules, and one draw needn't show every extreme that they name: `member_slot`: distinct over the 6144 rows. Slot s belongs to the block of device s // 768 in group+tile order; all rows of one cluster have slots in one group's 4 * 768 consecutive slots. Of the 384 rows of one device at most 48 have slots in one device's block, and in every draw the last device's block receives exactly 48 rows from every device. `member_cluster`: rows with equal values form a cluster.
All inputs are finite; a program needn't handle non-finite values.
Results may differ from a plain program's by a relative error of at most 0.00054.
Values may be sent and summed in bfloat16 or wider, within the bound.
No kernel may reach another device: no remote copies, remote signals or barrier semaphores. Data moves between devices by JAX's collectives and lax.ppermute only.
A program may use at most 64 MiB of HBM per device.

v0:
```python
import jax
import jax.numpy as jnp
from jax import lax
from jax.sharding import PartitionSpec as P


def decode_rows(code_rows, codebook):
    row_count, sub_count = code_rows.shape
    code_count, feature_width = codebook.shape
    sub_dim = feature_width // sub_count
    block_count = sub_count // 8
    tables = codebook.reshape(code_count, block_count, 8, sub_dim).transpose(1, 0, 2, 3)
    chosen = code_rows.reshape(row_count, block_count, 8).transpose(1, 0, 2)
    levels = lax.broadcasted_iota(jnp.int32, (1, 1, code_count), 2)

    def lookup(operands):
        table_block, chosen_block = operands
        one_hot = (chosen_block[:, :, None] == levels).astype(jnp.bfloat16)
        return jnp.einsum(
            "rsk,kse->rse", one_hot, table_block, preferred_element_type=jnp.float32
        ).reshape(row_count, 8 * sub_dim)

    pieces = lax.map(lookup, (tables, chosen))
    decoded = pieces.transpose(1, 0, 2).reshape(row_count, feature_width)
    inverse = lax.rsqrt(jnp.sum(decoded * decoded, axis=1, keepdims=True) + 1e-06)
    return (decoded * inverse).astype(jnp.bfloat16)


def best_scores(own_rows, own_ids, own_index, other_rows, other_ids, other_index):
    row_total = own_rows.shape[0]
    step_rows = 256
    stacked = (
        own_rows.reshape(row_total // step_rows, step_rows, own_rows.shape[1]),
        own_ids.reshape(row_total // step_rows, step_rows),
        own_index.reshape(row_total // step_rows, step_rows),
    )

    def score_block(operands):
        block_rows, block_ids, block_index = operands
        scores = lax.dot_general(
            block_rows, other_rows, (((1,), (1,)), ((), ())), preferred_element_type=jnp.float32
        )
        related = (block_ids[:, None] == other_ids[None, :]) & (block_ids[:, None] >= 0)
        row_best = jnp.max(
            jnp.where(related & (other_index[None, :] < block_index[:, None]), scores, -1.0), axis=1
        )
        return row_best

    return lax.map(score_block, stacked).reshape(row_total)


def body(product_codes, member_cluster, member_slot, codebook):
    row_count = product_codes.shape[0]
    block_rows = 2 * row_count
    group_count = lax.axis_size("group")
    tile_count = lax.axis_size("tile")
    devices = group_count * tile_count
    capacity = block_rows // devices
    buffer_rows = devices * capacity
    cargo = decode_rows(product_codes, codebook)
    cargo_width = cargo.shape[1]
    target = member_slot // block_rows
    local_slot = member_slot % block_rows
    row_pos = lax.broadcasted_iota(jnp.int32, (row_count, row_count), 0)
    column_pos = lax.broadcasted_iota(jnp.int32, (row_count, row_count), 1)
    order_rank = jnp.sum(
        ((target[:, None] == target[None, :]) & (column_pos < row_pos)).astype(jnp.int32), axis=1
    )
    position = target * capacity + order_rank
    send_cargo = jnp.zeros((buffer_rows, cargo_width), cargo.dtype).at[position].set(cargo)
    send_slot = jnp.full((buffer_rows,), -1, jnp.int32).at[position].set(local_slot)
    send_ids = jnp.full((buffer_rows,), -1, jnp.int32).at[position].set(member_cluster)
    recv_cargo, recv_slot, recv_ids = (
        lax.all_to_all(send_cargo, ("group", "tile"), split_axis=0, concat_axis=0, tiled=True),
        lax.all_to_all(send_slot, ("group", "tile"), split_axis=0, concat_axis=0, tiled=True),
        lax.all_to_all(send_ids, ("group", "tile"), split_axis=0, concat_axis=0, tiled=True),
    )
    placement = jnp.where(recv_slot >= 0, recv_slot, block_rows)
    member_cargo = (
        jnp.zeros((block_rows, cargo_width), cargo.dtype).at[placement].set(recv_cargo, mode="drop")
    )
    member_ids = jnp.full((block_rows,), -1, jnp.int32).at[placement].set(recv_ids, mode="drop")
    tile_here = lax.axis_index("tile")
    slot_range = lax.iota(jnp.int32, block_rows)
    own_index = tile_here * block_rows + slot_range
    floor_value = jnp.full((block_rows,), -1.0, jnp.float32)
    piece_cargo = lax.all_gather(member_cargo, "tile", axis=0, tiled=True)
    piece_ids = lax.all_gather(member_ids, "tile", axis=0, tiled=True)
    piece_index = lax.iota(jnp.int32, piece_cargo.shape[0])
    best_value = jnp.maximum(
        floor_value,
        best_scores(member_cargo, member_ids, own_index, piece_cargo, piece_ids, piece_index),
    )
    outgoing = best_value[jnp.where(recv_slot >= 0, recv_slot, 0)]
    incoming = lax.all_to_all(outgoing, ("group", "tile"), split_axis=0, concat_axis=0, tiled=True)
    return incoming[position]


def solution(mesh):
    placed = (
        P(("parts", "group", "tile"), None),
        P(("parts", "group", "tile")),
        P(("parts", "group", "tile")),
        P(),
    )
    return jax.shard_map(
        body, mesh=mesh, in_specs=placed, out_specs=P(("parts", "group", "tile")), check_vma=False
    )
```

profile of v0, /device:TPU:0, one launch (start us, length us, event | category | flops | bytes accessed | tf_op | source)
XLA Modules:
  0.0 163.7 jit_solution(451972846846259315)
XLA Ops:
  7.5 2.9 %scatter_custom_fusion = s32[768]{0:T(1024)S(1)} fusion(s32[384]{0:T(512)S(1)} %compare_select_fusion.4, s32[384]{0:T(512)S(1)} %get-tuple-element.128, s32[]{:T(128)} %constant.40.clone.1), kind=kCustom, calls=%fused_computation.58 | custom fusion | bytes 3076 | tf_op jit(solution)/shard_map/scatter | solution.py:71
  11.1 7.4 %all-to-all-start = ((s32[16,48,1]{1,2,0:T(1,128)}), s32[16,48,1]{1,2,0:T(1,128)S(1)}, u32[]{:S(2)}, u32[]{:S(2)}) async-start(s32[16,48,1]{1,2,0:T(1,128)} %bitcast), calls=%async_computation | async-start | bytes 16384 | tf_op jit(solution)/shard_map/all_to_all | solution.py:75
  19.6 23.2 %while.22 = (s32[]{:T(128)}, f32[12,384,64]{1,2,0:T(8,128)S(1)}, bf16[12,256,8,8]{1,3,2,0:T(8,128)(2,1)S(1)}, s32[12,384,8]{1,2,0:T(8,128)}, s32[]{:T(128)}) while((s32[]{:T(128)}, f32[12,384,64]{1,2,0:T(8,128)S(1)}, bf16[12,256,8,8]{1,3,2,0:T(8,128)(2,1)S(1)}, s32[12,384,8]{1,2,0:T(8,128)}, s32[]{:T(128)}) %tuple.52), condition=%wide.region_3.4_spmd.clone, body=%wide.region_2.3_spmd.clone.sunk | while | flops 13369346 | bytes 169025 | solution.py:23
  20.3 1.2 fusion.39
  22.3 1.2 fusion.39
  24.2 1.2 fusion.39
  26.1 1.2 fusion.39
  28.1 1.2 fusion.39
  30.0 1.2 fusion.39
  31.9 1.2 fusion.39
  33.9 1.2 fusion.39
  35.8 1.2 fusion.39
  37.7 1.2 fusion.39
  39.6 1.2 fusion.39
  43.3 3.1 %scatter_custom_fusion.3 = bf16[768,768]{1,0:T(8,128)(2,1)} fusion(s32[384]{0:T(512)S(1)} %compare_select_fusion.4, bf16[384,768]{1,0:T(8,128)(2,1)S(1)} %copy.18, bf16[]{:T(256)} %constant.39.clone.1), kind=kCustom, calls=%fused_computation.34 | custom fusion | bytes 1179650 | tf_op jit(solution)/shard_map/scatter | solution.py:70
  46.5 6.0 %all-to-all-start.2 = ((bf16[16,48,768]{2,1,0:T(8,128)(2,1)}), bf16[16,48,768]{2,1,0:T(8,128)(2,1)S(1)}, u32[]{:S(2)}, u32[]{:S(2)}) async-start(bf16[16,48,768]{2,1,0:T(8,128)(2,1)} %bitcast.9), calls=%async_computation.2 | async-start | bytes 2359296 | tf_op jit(solution)/shard_map/all_to_all | solution.py:74
  53.8 23.8 %all-to-all-done.2 = bf16[16,48,768]{2,1,0:T(8,128)(2,1)S(1)} async-done(((bf16[16,48,768]{2,1,0:T(8,128)(2,1)}), bf16[16,48,768]{2,1,0:T(8,128)(2,1)S(1)}, u32[]{:S(2)}, u32[]{:S(2)}) %all-to-all-start.2) | async-done | bytes 1179680 | tf_op jit(solution)/shard_map/all_to_all | solution.py:74
  77.6 6.7 %scatter_custom_fusion.4 = bf16[768,768]{1,0:T(8,128)(2,1)} fusion(s32[768]{0:T(1024)S(1)} %get-tuple-element.103, bf16[768,768]{1,0:T(8,128)(2,1)S(1)} %bitcast.60, bf16[]{:T(256)} %constant.39.clone.1), kind=kCustom, calls=%fused_computation.32 | custom fusion | bytes 1179650 | tf_op jit(solution)/shard_map/scatter | solution.py:80
  84.3 3.1 %scatter_custom_fusion.1 = s32[768]{0:T(1024)S(1)} fusion(s32[384]{0:T(512)S(1)} %compare_select_fusion.4, s32[384]{0:T(512)} %param.9, s32[]{:T(128)} %constant.40.clone.1), kind=kCustom, calls=%fused_computation.56 | custom fusion | bytes 3584 | tf_op jit(solution)/shard_map/scatter | solution.py:72
  88.1 7.5 %all-to-all-start.1 = ((s32[16,48,1]{1,2,0:T(1,128)}), s32[16,48,1]{1,2,0:T(1,128)S(1)}, u32[]{:S(2)}, u32[]{:S(2)}) async-start(s32[16,48,1]{1,2,0:T(1,128)} %bitcast.1), calls=%async_computation.1 | async-start | bytes 16384 | tf_op jit(solution)/shard_map/all_to_all | solution.py:76
  95.6 6.4 %all-to-all-done.1 = s32[16,48,1]{1,2,0:T(1,128)S(1)} async-done(((s32[16,48,1]{1,2,0:T(1,128)}), s32[16,48,1]{1,2,0:T(1,128)S(1)}, u32[]{:S(2)}, u32[]{:S(2)}) %all-to-all-start.1) | async-done | bytes 3104 | tf_op jit(solution)/shard_map/all_to_all | solution.py:76
  102.7 3.4 %scatter_custom_fusion.2 = s32[768]{0:T(1024)S(1)} fusion(s32[768]{0:T(1024)S(1)} %get-tuple-element.103, s32[768]{0:T(1024)S(1)} %reshape.144, s32[]{:T(128)} %constant.40.clone.1), kind=kCustom, calls=%fused_computation.54 | custom fusion | bytes 3076 | tf_op jit(solution)/shard_map/scatter | solution.py:82
  106.1 5.4 %all-gather = s32[4,1,768]{2,1,0:T(1,128)S(1)} all-gather(s32[1,1,768]{2,1,0:T(1,128)S(1)} %reshape.168), channel_id=1, replica_groups=mesh['parts'=2,'group'=4,'tile'=4] {'tile'}, dimensions={0}, use_global_device_ids=true | all-gather | bytes 15360 | tf_op jit(solution)/shard_map/all_gather | solution.py:88
  111.5 13.4 %all-gather.3.cloned.1.call-done = bf16[3072,768]{1,0:T(8,128)(2,1)} async-done(((bf16[768,768]{1,0:T(8,128)(2,1)}), bf16[3072,768]{1,0:T(8,128)(2,1)}) %all-gather.3.cloned.1.call-update) | async-done | bytes 4718608 | tf_op jit(solution)/shard_map/all_gather | solution.py:87
  124.9 12.6 %while.23 = (s32[]{:T(128)}, f32[3,256]{1,0:T(4,128)S(1)}, s32[3,256]{1,0:T(4,128)S(1)}, s32[3072]{0:T(1024)S(1)}, s32[3,256]{1,0:T(4,128)S(1)}, /*index=5*/bf16...) while((s32[]{:T(128)}, f32[3,256]{1,0:T(4,128)S(1)}, ...), condition=%wide.region_11.12_spmd.clone, body=%wide.region_9.11_spmd.clone.sunk | while | flops 1212678144 | bytes 5135461 | solution.py:49
  124.9 4.1 %fusion.42 = f32[256]{0:T(256)S(1)} fusion(bf16[3072,768]{1,0:T(8,128)(2,1)} %get-tuple-element.241, s32[256]{0:T(256)S(1)} %bitcast.64, pred[256]{0:T(512)(128)(4,1)S(1)} %broadcast_compare_fusion.2, s32[3072]{0:T(1024)S(1)} %get-tuple-element.238, s32[256]{0:T(256)S(1)} %bitcast.66, bf16[3,256,768]{2,1,0:T(8,128)(2,1)} %get-tuple-element.240, ...), kind=kOutput, calls=%fused_computation.21.clone.1 | convolution fusion | flops 1212677888 | bytes 5127936 | tf_op jit(solution)/shard_map/while/body/eval_jaxpr/dot_general | solution.py:40
  129.2 4.1 %fusion.42 = f32[256]{0:T(256)S(1)} fusion(bf16[3072,768]{1,0:T(8,128)(2,1)} %get-tuple-element.241, s32[256]{0:T(256)S(1)} %bitcast.64, pred[256]{0:T(512)(128)(4,1)S(1)} %broadcast_compare_fusion.2, s32[3072]{0:T(1024)S(1)} %get-tuple-element.238, s32[256]{0:T(256)S(1)} %bitcast.66, bf16[3,256,768]{2,1,0:T(8,128)(2,1)} %get-tuple-element.240, ...), kind=kOutput, calls=%fused_computation.21.clone.1 | convolution fusion | flops 1212677888 | bytes 5127936 | tf_op jit(solution)/shard_map/while/body/eval_jaxpr/dot_general | solution.py:40
  133.4 4.1 %fusion.42 = f32[256]{0:T(256)S(1)} fusion(bf16[3072,768]{1,0:T(8,128)(2,1)} %get-tuple-element.241, s32[256]{0:T(256)S(1)} %bitcast.64, pred[256]{0:T(512)(128)(4,1)S(1)} %broadcast_compare_fusion.2, s32[3072]{0:T(1024)S(1)} %get-tuple-element.238, s32[256]{0:T(256)S(1)} %bitcast.66, bf16[3,256,768]{2,1,0:T(8,128)(2,1)} %get-tuple-element.240, ...), kind=kOutput, calls=%fused_computation.21.clone.1 | convolution fusion | flops 1212677888 | bytes 5127936 | tf_op jit(solution)/shard_map/while/body/eval_jaxpr/dot_general | solution.py:40
  137.6 3.2 %gather_fusion = f32[768]{0:T(1024)S(1)} fusion(f32[768]{0:T(1024)S(1)} %max_broadcast_in_dim.7, s32[1024]{0:T(1024)S(1)} %pad_clamp_fusion.1), kind=kCustom, calls=%fused_computation | custom fusion | bytes 9216 | tf_op jit(solution)/shard_map/gather | solution.py:94
  141.4 4.7 %all-to-all-start.3 = ((f32[16,48,1]{1,2,0:T(1,128)}), f32[16,48,1]{1,2,0:T(1,128)S(1)}, u32[]{:S(2)}, u32[]{:S(2)}) async-start(f32[16,48,1]{1,2,0:T(1,128)} %bitcast.12), calls=%async_computation.3 | async-start | bytes 16384 | tf_op jit(solution)/shard_map/all_to_all | solution.py:95
  146.2 6.4 %all-to-all-done.3 = f32[16,48,1]{1,2,0:T(1,128)S(1)} async-done(((f32[16,48,1]{1,2,0:T(1,128)}), f32[16,48,1]{1,2,0:T(1,128)S(1)}, u32[]{:S(2)}, u32[]{:S(2)}) %all-to-all-start.3) | async-done | bytes 3104 | tf_op jit(solution)/shard_map/all_to_all | solution.py:95
  153.8 3.0 %gather_fusion.1 = f32[384]{0:T(512)} fusion(f32[768]{0:T(1024)S(1)} %all_to_all.43, s32[1024]{0:T(1024)S(1)} %pad_clamp_fusion), kind=kCustom, calls=%fused_computation.1 | custom fusion | bytes 4608 | tf_op jit(solution)/shard_map/gather | solution.py:96
  (54 shorter events, 17.9 us)
Async XLA Ops:
  11.1 35.4 %all-to-all-start = ((s32[16,48,1]{1,2,0:T(1,128)}), s32[16,48,1]{1,2,0:T(1,128)S(1)}, u32[]{:S(2)}, u32[]{:S(2)}) async-start(s32[16,48,1]{1,2,0:T(1,128)} %bitcast), calls=%async_computation | async-start | bytes 16384 | tf_op jit(solution)/shard_map/all_to_all | solution.py:75
  46.5 31.1 %all-to-all-start.2 = ((bf16[16,48,768]{2,1,0:T(8,128)(2,1)}), bf16[16,48,768]{2,1,0:T(8,128)(2,1)S(1)}, u32[]{:S(2)}, u32[]{:S(2)}) async-start(bf16[16,48,768]{2,1,0:T(8,128)(2,1)} %bitcast.9), calls=%async_computation.2 | async-start | bytes 2359296 | tf_op jit(solution)/shard_map/all_to_all | solution.py:74
  52.5 72.5 %all-gather.3.cloned.1.call-start = ((), (), s32[]{:S(2)}) async-start(), calls=%async_computation.4 | async-start | bytes 5898240 | tf_op jit(solution)/shard_map/all_gather | solution.py:87
  88.1 13.9 %all-to-all-start.1 = ((s32[16,48,1]{1,2,0:T(1,128)}), s32[16,48,1]{1,2,0:T(1,128)S(1)}, u32[]{:S(2)}, u32[]{:S(2)}) async-start(s32[16,48,1]{1,2,0:T(1,128)} %bitcast.1), calls=%async_computation.1 | async-start | bytes 16384 | tf_op jit(solution)/shard_map/all_to_all | solution.py:76
  141.4 11.1 %all-to-all-start.3 = ((f32[16,48,1]{1,2,0:T(1,128)}), f32[16,48,1]{1,2,0:T(1,128)S(1)}, u32[]{:S(2)}, u32[]{:S(2)}) async-start(f32[16,48,1]{1,2,0:T(1,128)} %bitcast.12), calls=%async_computation.3 | async-start | bytes 16384 | tf_op jit(solution)/shard_map/all_to_all | solution.py:95
Sparse Core Ops, SparseCore 0:
  84.5 40.4 all-gather.2
where the time goes:
time: 165 us; the launch traced here: 164 us
  waiting for transfers between devices  50.1 us (30%)
  local copies, waits for them, and re-layouts  38.9 us (24%)
  matrix products  26.9 us (16%)
  starting transfers between devices  25.6 us (16%)
  between operations  13.6 us (8%)
  blocking collectives  5.38 us (3%)
  other arithmetic  3.12 us (2%)
    all_to_all x1, waiting for transfers between devices, body(): lax.all_to_all(send_cargo, ('group', 'tile'), split_axis=0, concat_axis=0...  23.8 us
    dot_general x12, matrix products, lookup(): jnp.einsum('rsk,kse->rse', one_hot, table_block, preferred_element_type=j...  14.5 us
    all_gather x1, waiting for transfers between devices, body(): piece_cargo = lax.all_gather(member_cargo, 'tile', axis=0, tiled=True)  13.4 us
    dot_general x3, matrix products, score_block(): lax.dot_general(block_rows, other_rows, (((1,), (1,)), ((), ())), preferr...  12.4 us
    eq x12, local copies, waits for them, and re-layouts, lookup(): one_hot = (chosen_block[:, :, None] == levels).astype(jnp.bfloat16)  8.61 us
    all_to_all x1, starting transfers between devices, body(): lax.all_to_all(send_ids, ('group', 'tile'), split_axis=0, concat_axis=0,...  7.48 us
    all_to_all x1, starting transfers between devices, body(): lax.all_to_all(send_slot, ('group', 'tile'), split_axis=0, concat_axis=0,...  7.36 us
    scatter x1, local copies, waits for them, and re-layouts, body(): jnp.zeros((block_rows, cargo_width), cargo.dtype).at[placement]  6.72 us
  transfers between devices with their start and end apart: 5, of which 4 were waited for; matrix products, arithmetic and copies ran while one was open for 22% of the time, Pallas kernels for 0%

commit v1 on v0

v1 whole, which is shorter than its diff:
```python
import functools

import jax
import jax.numpy as jnp
from jax import lax
from jax.experimental import pallas as pl
from jax.experimental.pallas import tpu as pltpu
from jax.sharding import PartitionSpec as P

LANES = 128
META_ROWS = 16
STEP = 256
AXES = ("group", "tile")


def gather_lanes(table, index):
    return jnp.take_along_axis(table, index, axis=1, mode="promise_in_bounds")


def lookup(low, high, codes):
    index = codes & (LANES - 1)
    return jnp.where(codes < LANES, gather_lanes(low, index), gather_lanes(high, index))


def unpack(packed, codes_ref):
    blocks, _, rows = codes_ref.shape
    subs = blocks * 8
    codes_ref[...] = packed[:subs].astype(jnp.float32).astype(jnp.int32).reshape(blocks, 8, rows)
    meta = packed[subs:].astype(jnp.float32).astype(jnp.int32)
    key = ((meta[3:4] * 256 + meta[2:3]) * 256 + meta[1:2]) * 256 + meta[0:1]
    return key, key - (meta[5:6] * 256 + meta[4:5])


def inverse_norms(codes_ref, norms_ref, chunk):
    total = jnp.zeros((8, LANES), jnp.float32)
    for block in range(codes_ref.shape[0]):
        rows = slice(block * 8, block * 8 + 8)
        codes = codes_ref[block, :, chunk * LANES : (chunk + 1) * LANES]
        total += lookup(norms_ref[rows, :LANES], norms_ref[rows, LANES:], codes)
    return lax.rsqrt(jnp.sum(total, axis=0, keepdims=True) + 1e-06)


def decode(codes_ref, table_ref, norms_ref, out_ref, column0):
    blocks, _, rows = codes_ref.shape
    sub_dim = table_ref.shape[0] // (blocks * 8)
    chunks = rows // LANES
    inverse = [jnp.broadcast_to(inverse_norms(codes_ref, norms_ref, c), (sub_dim, LANES)) for c in range(chunks)]

    def block(b, carry):
        for pair in range(4):
            first = pl.multiple_of(b * 8 * sub_dim + pair * 2 * sub_dim, 2 * sub_dim)
            pieces = [[] for _ in range(chunks)]
            for half in range(2):
                table = table_ref[pl.ds(first + half * sub_dim, sub_dim), :]
                sub = pair * 2 + half
                for c in range(chunks):
                    codes = codes_ref[b, sub : sub + 1, c * LANES : (c + 1) * LANES]
                    codes = jnp.broadcast_to(codes, (sub_dim, LANES))
                    pieces[c].append(lookup(table[:, :LANES], table[:, LANES:], codes) * inverse[c])
            for c in range(chunks):
                lanes = slice(column0 + c * LANES, column0 + (c + 1) * LANES)
                out_ref[pl.ds(first, 2 * sub_dim), lanes] = jnp.concatenate(pieces[c], axis=0).astype(jnp.bfloat16)
        return carry

    lax.fori_loop(0, blocks, block, 0)


def table_kernel(codebook_ref, own_ref, table_ref, norms_ref, rows_ref, codes_ref):
    subs = norms_ref.shape[0]
    table = codebook_ref[...].astype(jnp.float32).T
    table_ref[...] = table
    norms_ref[...] = jnp.sum((table * table).reshape(subs, table.shape[0] // subs, table.shape[1]), axis=1)
    unpack(own_ref[...], codes_ref)
    decode(codes_ref, table_ref, norms_ref, rows_ref, 0)


def columns_kernel(first_core, *refs):
    refs = list(refs)
    own_ref = refs.pop(0) if first_core else None
    count = len(refs) - 6
    inputs = refs[:count]
    table_ref, norms_ref, out_ref, key_ref, codes_ref, wide_ref = refs[count:]
    rows = codes_ref.shape[2]
    for k in range(count):
        packed = inputs[k][...]
        if k == 0 and first_core:
            core = lax.rem(lax.axis_index("tile"), 2)
            packed = jnp.where(core == 0, own_ref[...], packed)
        key, _ = unpack(packed, codes_ref)
        decode(codes_ref, table_ref, norms_ref, wide_ref, 0)
        for c in range(rows // LANES):
            lanes = slice(c * LANES, (c + 1) * LANES)
            target = slice(k * rows + c * LANES, k * rows + (c + 1) * LANES)
            out_ref[target, :] = wide_ref[:, lanes].T
            key_ref[target, :] = jnp.broadcast_to(key[:, lanes], (LANES, LANES)).T


def score(rows_ref, key, base, columns_ref, column_key_ref, best_ref):
    count = rows_ref.shape[1]

    def step(j, best):
        first = pl.multiple_of(j * STEP, STEP)
        columns = columns_ref[pl.ds(first, STEP), :]
        column_key = column_key_ref[pl.ds(first, STEP), :]
        out = []
        for n in range(count // STEP):
            lanes = slice(n * STEP, (n + 1) * STEP)
            scores = jnp.dot(columns, rows_ref[:, lanes], preferred_element_type=jnp.float32)
            keys = jnp.concatenate([column_key] * (STEP // LANES), axis=1)
            allowed = (keys < key[:, lanes]) & (keys >= base[:, lanes])
            scores = jnp.where(allowed, scores, -1.0)
            out.append(jnp.maximum(best[n], jnp.max(scores.reshape(STEP // 8, 8, STEP), axis=0)))
        return tuple(out)

    start = tuple(jnp.full((8, STEP), -1.0, jnp.float32) for _ in range(count // STEP))
    best = lax.fori_loop(0, columns_ref.shape[0] // STEP, step, start)
    for n in range(count // STEP):
        best_ref[:, n * STEP : (n + 1) * STEP] = jnp.max(best[n], axis=0, keepdims=True)


def far_kernel(direct_ref, passed_ref, table_ref, norms_ref, columns_ref, column_key_ref, best_ref, codes_ref, rows_ref):
    core = lax.rem(lax.axis_index("tile"), 2)
    key, base = unpack(jnp.where(core == 0, direct_ref[...], passed_ref[...]), codes_ref)
    decode(codes_ref, table_ref, norms_ref, rows_ref, 0)
    score(rows_ref, key, base, columns_ref, column_key_ref, best_ref)


def near_kernel(own_ref, rows_ref, columns_ref, column_key_ref, best_ref):
    subs = own_ref.shape[0] - META_ROWS
    meta = own_ref[subs:, :].astype(jnp.float32).astype(jnp.int32)
    key = ((meta[3:4] * 256 + meta[2:3]) * 256 + meta[1:2]) * 256 + meta[0:1]
    base = key - (meta[5:6] * 256 + meta[4:5])
    score(rows_ref, key, base, columns_ref, column_key_ref, best_ref)


PARAMS = pltpu.CompilerParams(vmem_limit_bytes=48 * 1024 * 1024)


def body(product_codes, member_cluster, member_slot, codebook):
    row_count, subs = product_codes.shape
    code_count, features = codebook.shape
    groups = lax.axis_size("group")
    tiles = lax.axis_size("tile")
    devices = groups * tiles
    pair_rows = 2 * row_count
    group_slots = tiles * 2 * row_count
    core = lax.axis_index("tile") % 2

    def exchange(value, offset_core0, offset_core1):
        pairs = [(i, i ^ (offset_core0 if i % 2 == 0 else offset_core1)) for i in range(devices)]
        return lax.ppermute(value, AXES, pairs)

    far = (groups // 2) * tiles
    chips = [dz * tiles + dx * 2 for dz in range(groups // 2) for dx in range(tiles // 2)]
    half = len(chips) // 2
    first_chips, second_chips = chips[:half], chips[half:][::-1]

    local = member_slot % group_slots
    key = member_cluster * group_slots + local
    digits = [key & 255, (key >> 8) & 255, (key >> 16) & 255, key >> 24, local & 255, local >> 8]
    meta = jnp.stack(digits + [jnp.zeros_like(key)] * (META_ROWS - len(digits)))
    packed = jnp.concatenate([product_codes.T, meta]).astype(jnp.bfloat16)
    sibling = exchange(packed, 1, 1)
    own = jnp.concatenate(
        [jnp.where(core == 0, packed, sibling), jnp.where(core == 0, sibling, packed)], axis=1
    )
    arrived = [
        exchange(own, far if k == 0 else first_chips[k], second_chips[k]) for k in range(half)
    ]

    shape = jax.ShapeDtypeStruct
    codes_scratch = pltpu.VMEM((subs // 8, 8, pair_rows), jnp.int32)
    wide_scratch = pltpu.VMEM((features, pair_rows), jnp.bfloat16)
    table, norms, own_rows = pl.pallas_call(
        table_kernel,
        out_shape=(
            shape((features, code_count), jnp.float32),
            shape((subs, code_count), jnp.float32),
            shape((features, pair_rows), jnp.bfloat16),
        ),
        scratch_shapes=[codes_scratch],
        compiler_params=PARAMS,
        name="decode_own",
    )(codebook, own)
    passed = exchange(arrived[0], 1, 1)

    far_best, near_best = None, None
    for k in range(0, half, 2):
        batch = arrived[k : k + 2]
        columns, column_key = pl.pallas_call(
            functools.partial(columns_kernel, k == 0),
            out_shape=(
                shape((len(batch) * pair_rows, features), jnp.bfloat16),
                shape((len(batch) * pair_rows, LANES), jnp.int32),
            ),
            scratch_shapes=[codes_scratch, wide_scratch],
            compiler_params=PARAMS,
            name="decode_columns",
        )(*([own] if k == 0 else []), *batch, table, norms)
        far_part = pl.pallas_call(
            far_kernel,
            out_shape=shape((1, pair_rows), jnp.float32),
            scratch_shapes=[codes_scratch, wide_scratch],
            compiler_params=PARAMS,
            name="score_far",
        )(arrived[0], passed, table, norms, columns, column_key)
        near_part = pl.pallas_call(
            near_kernel,
            out_shape=shape((1, pair_rows), jnp.float32),
            compiler_params=PARAMS,
            name="score_near",
        )(own, own_rows, columns, column_key)
        far_best = far_part if far_best is None else jnp.maximum(far_best, far_part)
        near_best = near_part if near_best is None else jnp.maximum(near_best, near_part)

    total = jnp.maximum(near_best, exchange(far_best, far, far))
    first, second = total[:, :row_count], total[:, row_count:]
    keep = jnp.where(core == 0, first, second)
    other = exchange(jnp.where(core == 0, second, first), 1, 1)
    return jnp.maximum(keep, other).reshape(row_count)


def solution(mesh):
    placed = (
        P(("parts", "group", "tile"), None),
        P(("parts", "group", "tile")),
        P(("parts", "group", "tile")),
        P(),
    )
    return jax.shard_map(
        body, mesh=mesh, in_specs=placed, out_specs=P(("parts", "group", "tile")), check_vma=False
    )
```

time: 165 us -> 42.2 us (0.26)
  waiting for transfers between devices: 50.1 us -> 5.13 us
  local copies, waits for them, and re-layouts: 38.9 us -> 1.11 us
  matrix products: 26.9 us -> 0 us
  Pallas kernels: 0 us -> 23.6 us
  starting transfers between devices: 25.6 us -> 9.73 us
  between operations: 13.6 us -> 0.15 us
  blocking collectives: 5.38 us -> 0 us
    all_to_all x4 -> x0, waiting for transfers between devices: 36.6 us -> none  [the longest x1 23.8 us: body(): lax.all_to_all(send_cargo, ('group', 'tile'), split_axis=0, concat_axis=0...]
    dot_general x15 -> x0, matrix products: 26.9 us -> none  [the longest x12 14.5 us: lookup(): jnp.einsum('rsk,kse->rse', one_hot, table_block, preferred_element_type=j...]
    all_to_all x4 -> x0, starting transfers between devices: 25.6 us -> none  [the longest x1 7.48 us: body(): lax.all_to_all(send_ids, ('group', 'tile'), split_axis=0, concat_axis=0,...]
    pallas_call x0 -> x4, Pallas kernels: none -> 23.6 us  [the longest x1 9.13 us: body(): pl.pallas_call(functools.partial(columns_kernel, k == 0), out_shape=(shap...]
    scatter x5 -> x0, local copies, waits for them, and re-layouts: 19.2 us -> none  [the longest x1 6.72 us: body(): jnp.zeros((block_rows, cargo_width), cargo.dtype).at[placement]]
    all_gather x1 -> x0, waiting for transfers between devices: 13.4 us -> none  [body(): piece_cargo = lax.all_gather(member_cargo, 'tile', axis=0, tiled=True)]
    ppermute x0 -> x6, starting transfers between devices: none -> 9.73 us  [exchange(): return lax.ppermute(value, AXES, pairs)]
    eq x12 -> x0, local copies, waits for them, and re-layouts: 8.61 us -> none  [lookup(): one_hot = (chosen_block[:, :, None] == levels).astype(jnp.bfloat16)]
  transfers between devices with their start and end apart: 5 -> 6, of which waited for: 4 -> 3; matrix products, arithmetic and copies ran while one was open for 22% -> 0% of each run, Pallas kernels for 0% -> 39%
where the time goes in v1:
time: 42.2 us; the launch traced here: 42 us
  Pallas kernels  23.6 us (56%)
  starting transfers between devices  9.73 us (23%)
  waiting for transfers between devices  5.13 us (12%)
  other arithmetic  2.29 us (5%)
  local copies, waits for them, and re-layouts  1.11 us (3%)
    ppermute x6, starting transfers between devices, exchange(): return lax.ppermute(value, AXES, pairs)  9.73 us
    pallas_call x1, Pallas kernels, body(): pl.pallas_call(functools.partial(columns_kernel, k == 0), out_shape=(shap...  9.13 us
    pallas_call x1, Pallas kernels, body(): pl.pallas_call(far_kernel, out_shape=shape((1, pair_rows), jnp.float32),...  7.08 us
    ppermute x6, waiting for transfers between devices, exchange(): return lax.ppermute(value, AXES, pairs)  5.13 us
    pallas_call x1, Pallas kernels, body(): pl.pallas_call(table_kernel, out_shape=(shape((features, code_count), jnp...  4.34 us
    pallas_call x1, Pallas kernels, body(): pl.pallas_call(near_kernel, out_shape=shape((1, pair_rows), jnp.float32),...  3.01 us
    unnamed x2, local copies, waits for them, and re-layouts  1 us
    transpose x1, other arithmetic, body(): packed = jnp.concatenate([product_codes.T, meta]).astype(jnp.bfloat16)  0.92 us
  transfers between devices with their start and end apart: 6, of which 3 were waited for; matrix products, arithmetic and copies ran while one was open for 0% of the time, Pallas kernels for 39%

profile of v1, /device:TPU:0, one launch (start us, length us, event | category | flops | bytes accessed | tf_op | source)
XLA Modules:
  0.0 42.0 jit_solution(17450109390712065595)
XLA Ops:
  0.0 0.9 %convert_bitcast_fusion = bf16[96,384]{1,0:T(8,128)(2,1)S(1)} fusion(s32[384,96]{0,1:T(8,128)} %param.4), kind=kLoop, calls=%fused_computation.3 | loop fusion | flops 36864 | bytes 221184 | tf_op jit(solution)/shard_map/transpose | solution.py:162
  0.9 0.7 %shift-right-arithmetic_convert_fusion = (bf16[384]{0:T(512)(128)(2,1)S(1)}, bf16[384]{0:T(512)(128)(2,1)S(1)}, bf16[384]{0:T(512)(128)(2,1)S(1)}, s32[384]{0:T(512)S(1)}) fusion(s32[384]{0:T(512)} %param.6, s32[384]{0:T(512)} %param.5), kind=kLoop, calls=%fused_computation.7 | loop fusion | flops 5376 | bytes 6912 | tf_op jit(solution)/shard_map/convert.9
  1.7 0.1 concatenate.15
  1.8 0.5 %collective-permute-start = (bf16[112,384]{1,0:T(8,128)(2,1)S(1)}, bf16[112,384]{1,0:T(8,128)(2,1)S(1)}, u32[]{:S(2)}, u32[]{:S(2)}) collective-permute-start(bf16[112,384]{1,0:T(8,128)(2,1)S(1)} %concatenate.15), channel_id=1, source_target_pairs={{0,1},{1,0},{2,3},{3,2},{4,5},{5,4},{6,7},{7,6},{8,9},{9,8},{10,11... | collective-permute-start | bytes 258056 | tf_op jit(solution)/shard_map/ppermute | solution.py:151
  2.3 0.9 %collective-permute-done = bf16[112,384]{1,0:T(8,128)(2,1)S(1)} collective-permute-done((bf16[112,384]{1,0:T(8,128)(2,1)S(1)}, bf16[112,384]{1,0:T(8,128)(2,1)S(1)}, u32[]{:S(2)}, u32[]{:S(2)}) %collective-permute-start) | collective-permute-done | bytes 86048 | tf_op jit(solution)/shard_map/ppermute | solution.py:151
  3.3 4.0 %collective-permute-start.1 = (bf16[112,768]{1,0:T(8,128)(2,1)S(1)}, bf16[112,768]{1,0:T(8,128)(2,1)S(1)}, u32[]{:S(2)}, u32[]{:S(2)}) collective-permute-start(bf16[112,768]{1,0:T(8,128)(2,1)S(1)} %pad_maximum_fusion.own_ref.refs_0_), channel_id=1, source_target_pairs={{0,8},{1,7},{2,10},{3,5},{4,12},{5,3},{6,14},{7,1},{8,0},{9,15},{1... | collective-permute-start | bytes 516104 | tf_op jit(solution)/shard_map/ppermute | solution.py:151
  7.3 1.5 %collective-permute-start.2 = (bf16[112,768]{1,0:T(8,128)(2,1)S(1)}, bf16[112,768]{1,0:T(8,128)(2,1)S(1)}, u32[]{:S(2)}, u32[]{:S(2)}) collective-permute-start(bf16[112,768]{1,0:T(8,128)(2,1)S(1)} %pad_maximum_fusion.own_ref.refs_0_), channel_id=1, source_target_pairs={{0,2},{1,5},{2,0},{3,7},{4,6},{5,1},{6,4},{7,3},{8,10},{9,13},{10,... | collective-permute-start | bytes 516104 | tf_op jit(solution)/shard_map/ppermute | solution.py:151
  8.8 3.3 %collective-permute-done.1.refs_1_.direct_ref = bf16[112,768]{1,0:T(8,128)(2,1)S(1)} collective-permute-done((bf16[112,768]{1,0:T(8,128)(2,1)S(1)}, bf16[112,768]{1,0:T(8,128)(2,1)S(1)}, u32[]{:S(2)}, u32[]{:S(2)}) %collective-permute-start.1) | collective-permute-done | bytes 172064 | tf_op jit(solution)/shard_map/ppermute | solution.py:151
  12.1 0.0 collective-permute-start.3
  12.1 0.0 copy-start
  12.1 1.0 %copy-done = bf16[256,768]{1,0:T(8,128)(2,1)S(1)} copy-done((bf16[256,768]{1,0:T(8,128)(2,1)S(1)}, bf16[256,768]{1,0:T(8,128)(2,1)}, u32[]{:S(2)}) %copy-start) | copy-done | bytes 393240
  13.1 4.3 %decode_own.1 = (f32[768,256]{1,0:T(8,128)S(1)}, f32[96,256]{1,0:T(8,128)S(1)}, bf16[768,768]{1,0:T(8,128)(2,1)S(1)}) custom-call(bf16[256,768]{1,0:T(8,128)(2,1)S(1)} %copy-done, bf16[112,768]{1,0:T(8,128)(2,1)S(1)} %pad_maximum_fusion.own_ref.refs_0_), custom_call_target="tpu_custom_call" | custom-call | tf_op jit(solution)/shard_map/decode_own/pallas_call | solution.py:174
  17.4 0.0 collective-permute-done.2.refs_2_
  17.4 9.1 %decode_columns.1 = (bf16[1536,768]{1,0:T(8,128)(2,1)S(1)}, s32[1536,128]{1,0:T(8,128)S(1)}) custom-call(bf16[112,768]{1,0:T(8,128)(2,1)S(1)} %pad_maximum_fusion.own_ref.refs_0_, bf16[112,768]{1,0:T(8,128)(2,1)S(1)} %collective-permute-done.1.refs_1_.direct_ref, bf16[112,768]{1,0:T(8,128)(2,1)S(1)} %collective-permute-done.2.refs_2_, ...), custom_call_target="tpu_custom_call" | custom-call | tf_op jit(solution)/shard_map/decode_columns/pallas_call | solution.py:190
  26.6 0.0 collective-permute-done.3.passed_ref
  26.6 7.1 %score_far.1 = f32[1,768]{1,0:T(1,128)S(1)} custom-call(bf16[112,768]{1,0:T(8,128)(2,1)S(1)} %collective-permute-done.1.refs_1_.direct_ref, bf16[112,768]{1,0:T(8,128)(2,1)S(1)} %collective-permute-done.3.passed_ref, f32[768,256]{1,0:T(8,128)S(1)} %get-tuple-element.11.refs_3_.table_ref, f32[96,256]{1,0:T(8,128)S(1)} %get-tuple-element.12.refs_4_.norms_ref, ...), custom_call_target="tpu_custom_call" | custom-call | tf_op jit(solution)/shard_map/score_far/pallas_call | solution.py:200
  33.6 3.4 %collective-permute-start.4 = (f32[1,768]{1,0:T(1,128)S(1)}, f32[1,768]{1,0:T(1,128)S(1)}, u32[]{:S(2)}, u32[]{:S(2)}) collective-permute-start(f32[1,768]{1,0:T(1,128)S(1)} %score_far.1), channel_id=1, source_target_pairs={{0,8},{1,9},{2,10},{3,11},{4,12},{5,13},{6,14},{7,15},{8,0},{9,1},... | collective-permute-start | bytes 9224 | tf_op jit(solution)/shard_map/ppermute | solution.py:151
  37.1 3.0 %score_near.1 = f32[1,768]{1,0:T(1,128)S(1)} custom-call(bf16[112,768]{1,0:T(8,128)(2,1)S(1)} %pad_maximum_fusion.own_ref.refs_0_, bf16[768,768]{1,0:T(8,128)(2,1)S(1)} %get-tuple-element.10.rows_ref, bf16[1536,768]{1,0:T(8,128)(2,1)S(1)} %get-tuple-element.13.columns_ref, s32[1536,128]{1,0:T(8,128)S(1)} %get-tuple-element.14.column_key_ref), custom_call_target="tpu_custom_call" | custom-call | tf_op jit(solution)/shard_map/score_near/pallas_call | solution.py:207
  40.1 0.0 collective-permute-done.4
  40.1 0.3 collective-permute-start.5
  40.4 0.9 %collective-permute-done.5 = f32[1,384]{1,0:T(1,128)S(1)} collective-permute-done((f32[1,384]{1,0:T(1,128)S(1)}, f32[1,384]{1,0:T(1,128)S(1)}, u32[]{:S(2)}, u32[]{:S(2)}) %collective-permute-start.5) | collective-permute-done | bytes 1568 | tf_op jit(solution)/shard_map/ppermute | solution.py:151
  41.4 0.6 %fusion.1 = f32[384]{0:T(512)} fusion(f32[1,384]{1,0:T(1,128)S(1)} %collective-permute-done.5, pred[]{:T(512)S(6)} %eq.6, f32[1,768]{1,0:T(1,128)S(1)} %max.6), kind=kLoop, calls=%fused_computation.15 | loop fusion | flops 768 | bytes 6145 | tf_op jit(solution)/shard_map/max | solution.py:220
  (13 shorter events, 0.1 us)
Async XLA Ops:
  1.8 1.4 %collective-permute-start = (bf16[112,384]{1,0:T(8,128)(2,1)S(1)}, bf16[112,384]{1,0:T(8,128)(2,1)S(1)}, u32[]{:S(2)}, u32[]{:S(2)}) collective-permute-start(bf16[112,384]{1,0:T(8,128)(2,1)S(1)} %concatenate.15), channel_id=1, source_target_pairs={{0,1},{1,0},{2,3},{3,2},{4,5},{5,4},{6,7},{7,6},{8,9},{9,8},{10,11... | collective-permute-start | bytes 258056 | tf_op jit(solution)/shard_map/ppermute | solution.py:151
  3.3 8.8 %collective-permute-start.1 = (bf16[112,768]{1,0:T(8,128)(2,1)S(1)}, bf16[112,768]{1,0:T(8,128)(2,1)S(1)}, u32[]{:S(2)}, u32[]{:S(2)}) collective-permute-start(bf16[112,768]{1,0:T(8,128)(2,1)S(1)} %pad_maximum_fusion.own_ref.refs_0_), channel_id=1, source_target_pairs={{0,8},{1,7},{2,10},{3,5},{4,12},{5,3},{6,14},{7,1},{8,0},{9,15},{1... | collective-permute-start | bytes 516104 | tf_op jit(solution)/shard_map/ppermute | solution.py:151
  7.3 10.1 %collective-permute-start.2 = (bf16[112,768]{1,0:T(8,128)(2,1)S(1)}, bf16[112,768]{1,0:T(8,128)(2,1)S(1)}, u32[]{:S(2)}, u32[]{:S(2)}) collective-permute-start(bf16[112,768]{1,0:T(8,128)(2,1)S(1)} %pad_maximum_fusion.own_ref.refs_0_), channel_id=1, source_target_pairs={{0,2},{1,5},{2,0},{3,7},{4,6},{5,1},{6,4},{7,3},{8,10},{9,13},{10,... | collective-permute-start | bytes 516104 | tf_op jit(solution)/shard_map/ppermute | solution.py:151
  12.1 14.5 %collective-permute-start.3 = (bf16[112,768]{1,0:T(8,128)(2,1)S(1)}, bf16[112,768]{1,0:T(8,128)(2,1)S(1)}, u32[]{:S(2)}, u32[]{:S(2)}) collective-permute-start(bf16[112,768]{1,0:T(8,128)(2,1)S(1)} %collective-permute-done.1.refs_1_.direct_ref), channel_id=1, source_target_pairs={{0,1},{1,0},{2,3},{3,2},{4,5},{5,4},{6,7},{7,6},{8,9},{9,8},{10,11... | collective-permute-start | bytes 516104 | tf_op jit(solution)/shard_map/ppermute | solution.py:151
  12.1 1.0 %copy-start = (bf16[256,768]{1,0:T(8,128)(2,1)S(1)}, bf16[256,768]{1,0:T(8,128)(2,1)}, u32[]{:S(2)}) copy-start(bf16[256,768]{1,0:T(8,128)(2,1)} %codebook_ref.1) | copy-start | bytes 1179652
  33.6 6.5 %collective-permute-start.4 = (f32[1,768]{1,0:T(1,128)S(1)}, f32[1,768]{1,0:T(1,128)S(1)}, u32[]{:S(2)}, u32[]{:S(2)}) collective-permute-start(f32[1,768]{1,0:T(1,128)S(1)} %score_far.1), channel_id=1, source_target_pairs={{0,8},{1,9},{2,10},{3,11},{4,12},{5,13},{6,14},{7,15},{8,0},{9,1},... | collective-permute-start | bytes 9224 | tf_op jit(solution)/shard_map/ppermute | solution.py:151
  40.1 1.2 %collective-permute-start.5 = (f32[1,384]{1,0:T(1,128)S(1)}, f32[1,384]{1,0:T(1,128)S(1)}, u32[]{:S(2)}, u32[]{:S(2)}) collective-permute-start(f32[1,384]{1,0:T(1,128)S(1)} %broadcast_select_fusion.2), channel_id=1, source_target_pairs={{0,1},{1,0},{2,3},{3,2},{4,5},{5,4},{6,7},{7,6},{8,9},{9,8},{10,11... | collective-permute-start | bytes 4616 | tf_op jit(solution)/shard_map/ppermute | solution.py:151

commit v2 on v0

v2 whole, which is shorter than its diff:
```python
import functools

import jax
import jax.numpy as jnp
from jax import lax
from jax.experimental import pallas as pl
from jax.experimental.pallas import tpu as pltpu
from jax.sharding import PartitionSpec as P

LANES = 128
META_ROWS = 16
BLOCK_SUBS = 16
STEP_ROWS = 768
STEP_LANES = 256
AXES = ("group", "tile")
GATHER = lax.GatherDimensionNumbers(
    offset_dims=(),
    collapsed_slice_dims=(1,),
    start_index_map=(1,),
    operand_batching_dims=(0,),
    start_indices_batching_dims=(0,),
)


def core_index():
    return lax.rem(lax.axis_index("tile"), 2)


def gather_lanes(table, index):
    return lax.gather(
        table, index[..., None], GATHER, slice_sizes=(1, 1), mode=lax.GatherScatterMode.PROMISE_IN_BOUNDS
    )


def integers(values):
    return values.astype(jnp.float32).astype(jnp.int32)


def read_keys(meta):
    meta = integers(meta)
    key = ((meta[3:4] * 256 + meta[2:3]) * 256 + meta[1:2]) * 256 + meta[0:1]
    return key, key - (meta[5:6] * 256 + meta[4:5])


def spread_keys(key, out_ref):
    for c in range(key.shape[1] // LANES):
        lanes = slice(c * LANES, (c + 1) * LANES)
        out_ref[lanes, :] = jnp.broadcast_to(key[:, lanes], (LANES, LANES)).T


def make_table(codebook_ref, table_ref, wide_ref, sub_dim):
    features = table_ref.shape[0]
    wide = codebook_ref[...].astype(jnp.float32).T
    for half in range(wide.shape[1] // LANES):
        lanes = slice(half * LANES, (half + 1) * LANES)
        wide_ref[...] = wide[:, lanes]
        for first in range(0, features, BLOCK_SUBS * sub_dim):
            for e in range(sub_dim):
                row = first + e * BLOCK_SUBS
                strided = wide_ref[pl.ds(first + e, BLOCK_SUBS, stride=sub_dim), :]
                table_ref[row : row + BLOCK_SUBS, lanes] = strided.astype(jnp.bfloat16)


def decode(codes, table_ref, exact_ref, out_ref):
    features = table_ref.shape[0]
    subs, rows = codes.shape
    sub_dim = features // subs
    for c in range(rows // LANES):
        lanes = slice(c * LANES, (c + 1) * LANES)
        total = jnp.zeros((8, LANES), jnp.float32)
        for block in range(subs // BLOCK_SUBS):
            chosen = integers(codes[block * BLOCK_SUBS : (block + 1) * BLOCK_SUBS, lanes]).astype(jnp.int16)
            index = chosen & (LANES - 1)
            in_low = chosen < LANES
            for e in range(sub_dim):
                row = (block * sub_dim + e) * BLOCK_SUBS
                table = table_ref[row : row + BLOCK_SUBS, :]
                low, high = gather_lanes(table[:, :LANES], index), gather_lanes(table[:, LANES:], index)
                exact = jnp.where(in_low, low, high)
                exact_ref[row : row + BLOCK_SUBS, lanes] = exact
                square = exact.astype(jnp.float32)
                square = square * square
                total = total + square[:8] + square[8:]
        inverse = lax.rsqrt(jnp.sum(total, axis=0, keepdims=True) + 1e-06)
        inverse = jnp.broadcast_to(inverse, (BLOCK_SUBS, LANES))
        for row in range(0, features, BLOCK_SUBS):
            exact = exact_ref[row : row + BLOCK_SUBS, lanes].astype(jnp.float32)
            out_ref[row : row + BLOCK_SUBS, lanes] = (exact * inverse).astype(jnp.bfloat16)


def meta_rows(cluster, slot, group_slots, groups):
    local = slot
    for g in range(1, groups):
        local = local - jnp.where(slot >= g * group_slots, group_slots, 0)
    key = cluster * group_slots + local
    digits = [key & 255, (key >> 8) & 255, (key >> 16) & 255, key >> 24, local & 255, local >> 8]
    row = lax.broadcasted_iota(jnp.int32, (META_ROWS, key.shape[1]), 0)
    meta = jnp.zeros(row.shape, jnp.int32)
    for d, digit in enumerate(digits):
        meta = jnp.where(row == d, digit, meta)
    return meta.astype(jnp.float32).astype(jnp.bfloat16)


def pack_kernel(group_slots, groups, codes_ref, cluster_ref, slot_ref, out_ref):
    subs, rows = codes_ref.shape
    out_ref[:subs, :] = codes_ref[...].astype(jnp.float32).astype(jnp.bfloat16)
    cluster, slot = cluster_ref[...].reshape(1, rows), slot_ref[...].reshape(1, rows)
    out_ref[subs:, :] = meta_rows(cluster, slot, group_slots, groups)


def join_kernel(group_slots, groups, packed_ref, codes_ref, cluster_ref, slot_ref, out_ref, other_ref):
    rows = packed_ref.shape[1]
    pack_kernel(group_slots, groups, codes_ref, cluster_ref, slot_ref, other_ref)
    first = core_index() == 0
    out_ref[:, :rows] = jnp.where(first, packed_ref[...], other_ref[...])
    out_ref[:, rows:] = jnp.where(first, other_ref[...], packed_ref[...])


def own_kernel(codebook_ref, packed_ref, table_ref, rows_ref, wide_ref, exact_ref):
    subs = packed_ref.shape[0] - META_ROWS
    make_table(codebook_ref, table_ref, wide_ref, codebook_ref.shape[1] // subs)
    decode(packed_ref[:subs, :], table_ref, exact_ref, rows_ref)


def columns_kernel(with_own, *refs):
    refs = list(refs)
    own_ref, own_rows_ref = (refs.pop(0), refs.pop(0)) if with_own else (None, None)
    packed_ref, table_ref, out_ref, key_ref, exact_ref, rows_ref = refs
    subs = packed_ref.shape[0] - META_ROWS
    decode(packed_ref[:subs, :], table_ref, exact_ref, rows_ref)
    if with_own:
        first = core_index() == 0
        out_ref[...] = jnp.where(first, own_rows_ref[...], rows_ref[...]).T
        key, _ = read_keys(jnp.where(first, own_ref[subs:, :], packed_ref[subs:, :]))
    else:
        out_ref[...] = rows_ref[...].T
        key, _ = read_keys(packed_ref[subs:, :])
    spread_keys(key, key_ref)


def score(rows_ref, meta, pairs, best_ref, so_far_ref=None):
    key, base = read_keys(meta)
    for n in range(rows_ref.shape[1] // STEP_LANES):
        lanes = slice(n * STEP_LANES, (n + 1) * STEP_LANES)
        best = jnp.full((8, STEP_LANES), -1.0, jnp.float32)
        for columns_ref, column_key_ref in pairs:
            for first in range(0, columns_ref.shape[0], STEP_ROWS):
                span = slice(first, first + STEP_ROWS)
                scores = jnp.dot(columns_ref[span, :], rows_ref[:, lanes], preferred_element_type=jnp.float32)
                keys = jnp.concatenate([column_key_ref[span, :]] * (STEP_LANES // LANES), axis=1)
                allowed = (keys < key[:, lanes]) & (keys >= base[:, lanes])
                scores = jnp.where(allowed, scores, -1.0)
                best = jnp.maximum(best, jnp.max(scores.reshape(STEP_ROWS // 8, 8, STEP_LANES), axis=0))
        best = jnp.max(best, axis=0, keepdims=True)
        best_ref[:, lanes] = best if so_far_ref is None else jnp.maximum(best, so_far_ref[:, lanes])


def far_first_kernel(
    direct_ref, passed_ref, table_ref, columns_ref, key_ref, meta_ref, rows_ref, best_ref, exact_ref
):
    subs = direct_ref.shape[0] - META_ROWS
    packed = jnp.where(core_index() == 0, direct_ref[...], passed_ref[...])
    meta_ref[...] = packed[subs:]
    decode(packed[:subs], table_ref, exact_ref, rows_ref)
    score(rows_ref, packed[subs:], [(columns_ref, key_ref)], best_ref)


def far_kernel(
    packed_ref, table_ref, meta_ref, far_rows_ref, so_far_ref, columns_ref, key_ref, best_ref, exact_ref, rows_ref
):
    columns_kernel(False, packed_ref, table_ref, columns_ref, key_ref, exact_ref, rows_ref)
    score(far_rows_ref, meta_ref[...], [(columns_ref, key_ref)], best_ref, so_far_ref)


def near_kernel(own_ref, rows_ref, *refs):
    *refs, best_ref = refs
    subs = own_ref.shape[0] - META_ROWS
    score(rows_ref, own_ref[subs:, :], list(zip(refs[::2], refs[1::2])), best_ref)


def call(kernel, microseconds, name, out_shape, scratch=()):
    return pl.pallas_call(
        kernel,
        out_shape=out_shape,
        scratch_shapes=scratch,
        compiler_params=pltpu.CompilerParams(vmem_limit_bytes=24 * 1024 * 1024),
        cost_estimate=pl.CostEstimate(flops=int(microseconds * 1.15e9), bytes_accessed=0, transcendentals=0),
        name=name,
    )


def body(product_codes, member_cluster, member_slot, codebook):
    row_count, subs = product_codes.shape
    code_count, features = codebook.shape
    groups = lax.axis_size("group")
    tiles = lax.axis_size("tile")
    devices = groups * tiles
    pair_rows = 2 * row_count
    group_slots = tiles * 2 * row_count
    packed_rows = subs + META_ROWS
    core = core_index()

    def exchange(value, offset_core0, offset_core1):
        pairs = [(i, i ^ (offset_core0 if i % 2 == 0 else offset_core1)) for i in range(devices)]
        return lax.ppermute(value, AXES, pairs)

    far = (groups // 2) * tiles
    chips = [dz * tiles + dx * 2 for dz in range(groups // 2) for dx in range(tiles // 2)]
    half = len(chips) // 2
    first_chips, second_chips = chips[:half], chips[half:]

    shape = jax.ShapeDtypeStruct
    bf16 = jnp.bfloat16
    exact_scratch = pltpu.VMEM((features, pair_rows), bf16)
    rows_shape = shape((features, pair_rows), bf16)
    columns_shape = shape((pair_rows, features), bf16)
    key_shape = shape((pair_rows, LANES), jnp.int32)
    best_shape = shape((1, pair_rows), jnp.float32)

    mine = (product_codes, member_cluster, member_slot)
    other_codes, other_cluster, other_slot = (exchange(value, 1, 1) for value in mine)
    packed = call(
        functools.partial(pack_kernel, group_slots, groups), 0.3, "pack", shape((packed_rows, row_count), bf16)
    )(product_codes.T, member_cluster, member_slot)
    own = call(
        functools.partial(join_kernel, group_slots, groups),
        0.3,
        "join",
        shape((packed_rows, pair_rows), bf16),
        [pltpu.VMEM((packed_rows, row_count), bf16)],
    )(packed, other_codes.T, other_cluster, other_slot)
    arrived = [exchange(own, far if k == 0 else first_chips[k], second_chips[k]) for k in range(half)]

    table, own_rows = call(
        own_kernel,
        1.2,
        "decode_own",
        (shape((features, code_count), bf16), rows_shape),
        [pltpu.VMEM((features, LANES), jnp.float32), exact_scratch],
    )(codebook, own)
    arrived[0], table = lax.optimization_barrier((arrived[0], table))
    passed = exchange(arrived[0], 1, 1)
    columns = call(
        functools.partial(columns_kernel, True),
        1.2,
        "columns_first",
        (columns_shape, key_shape),
        [exact_scratch, exact_scratch],
    )(own, own_rows, arrived[0], table)
    far_meta, far_rows, far_best = call(
        far_first_kernel,
        2.0,
        "far_first",
        (shape((META_ROWS, pair_rows), bf16), rows_shape, best_shape),
        [exact_scratch],
    )(arrived[0], passed, table, *columns)
    columns = [columns]
    for k in range(1, half):
        *latest, far_best = call(
            far_kernel, 2.0, "far_next", (columns_shape, key_shape, best_shape), [exact_scratch, exact_scratch]
        )(arrived[k], table, far_meta, far_rows, far_best)
        columns.append(latest)
    returned = exchange(far_best, far, far)
    near_best = None
    for k in range(0, half, 2):
        operands = [array for pair in columns[k : k + 2] for array in pair]
        part = call(near_kernel, 2.0, "near", best_shape)(own, own_rows, *operands)
        near_best = part if near_best is None else jnp.maximum(near_best, part)

    total = jnp.maximum(near_best, returned)
    first, second = total[:, :row_count], total[:, row_count:]
    keep = jnp.where(core == 0, first, second)
    other = exchange(jnp.where(core == 0, second, first), 1, 1)
    return jnp.maximum(keep, other).reshape(row_count)


def solution(mesh):
    placed = (
        P(("parts", "group", "tile"), None),
        P(("parts", "group", "tile")),
        P(("parts", "group", "tile")),
        P(),
    )
    return jax.shard_map(
        body, mesh=mesh, in_specs=placed, out_specs=P(("parts", "group", "tile")), check_vma=False
    )
```

time: 165 us -> 28.2 us (0.17)
  waiting for transfers between devices: 50.1 us -> 4.99 us
  local copies, waits for them, and re-layouts: 38.9 us -> 2.28 us
  matrix products: 26.9 us -> 0 us
  starting transfers between devices: 25.6 us -> 10.1 us
  between operations: 13.6 us -> 0.1 us
  Pallas kernels: 0 us -> 9.99 us
  blocking collectives: 5.38 us -> 0 us
  other arithmetic: 3.12 us -> 0.61 us
    all_to_all x4 -> x0, waiting for transfers between devices: 36.6 us -> none  [the longest x1 23.8 us: body(): lax.all_to_all(send_cargo, ('group', 'tile'), split_axis=0, concat_axis=0...]
    dot_general x15 -> x0, matrix products: 26.9 us -> none  [the longest x12 14.5 us: lookup(): jnp.einsum('rsk,kse->rse', one_hot, table_block, preferred_element_type=j...]
    all_to_all x4 -> x0, starting transfers between devices: 25.6 us -> none  [the longest x1 7.48 us: body(): lax.all_to_all(send_ids, ('group', 'tile'), split_axis=0, concat_axis=0,...]
    scatter x5 -> x0, local copies, waits for them, and re-layouts: 19.2 us -> none  [the longest x1 6.72 us: body(): jnp.zeros((block_rows, cargo_width), cargo.dtype).at[placement]]
    all_gather x1 -> x0, waiting for transfers between devices: 13.4 us -> none  [body(): piece_cargo = lax.all_gather(member_cargo, 'tile', axis=0, tiled=True)]
    ppermute x0 -> x8, starting transfers between devices: none -> 10.1 us  [exchange(): return lax.ppermute(value, AXES, pairs)]
    pallas_call x0 -> x7, Pallas kernels: none -> 9.99 us  [the longest x1 2.68 us: body(): call(far_kernel, 2.0, 'far_next', (columns_shape, key_shape, best_shape),...]
    eq x12 -> x0, local copies, waits for them, and re-layouts: 8.61 us -> none  [lookup(): one_hot = (chosen_block[:, :, None] == levels).astype(jnp.bfloat16)]
  transfers between devices with their start and end apart: 5 -> 8, of which waited for: 4 -> 3; matrix products, arithmetic and copies ran while one was open for 22% -> 0% of each run, Pallas kernels for 0% -> 26%
where the time goes in v2:
time: 28.2 us; the launch traced here: 28 us
  starting transfers between devices  10.1 us (36%)
  Pallas kernels  9.99 us (35%)
  waiting for transfers between devices  4.99 us (18%)
  local copies, waits for them, and re-layouts  2.28 us (8%)
  other arithmetic  0.61 us (2%)
    ppermute x8, starting transfers between devices, exchange(): return lax.ppermute(value, AXES, pairs)  10.1 us
    ppermute x8, waiting for transfers between devices, exchange(): return lax.ppermute(value, AXES, pairs)  4.99 us
    pallas_call x1, Pallas kernels, body(): call(far_kernel, 2.0, 'far_next', (columns_shape, key_shape, best_shape),...  2.68 us
    pallas_call x1, Pallas kernels, body(): call(far_first_kernel, 2.0, 'far_first', (shape((META_ROWS, pair_rows), b...  2.55 us
    unnamed x8, local copies, waits for them, and re-layouts  2.28 us
    pallas_call x1, Pallas kernels, body(): part = call(near_kernel, 2.0, 'near', best_shape)(own, own_rows, *operands)  2.14 us
    pallas_call x1, Pallas kernels, body(): call(functools.partial(columns_kernel, True), 1.2, 'columns_first', (colu...  1.43 us
    pallas_call x1, Pallas kernels, body(): call(own_kernel, 1.2, 'decode_own', (shape((features, code_count), bf16),...  1.12 us
  transfers between devices with their start and end apart: 8, of which 3 were waited for; matrix products, arithmetic and copies ran while one was open for 0% of the time, Pallas kernels for 26%

profile of v2, /device:TPU:0, one launch (start us, length us, event | category | flops | bytes accessed | tf_op | source)
XLA Modules:
  0.0 28.0 jit_solution(11642009878812743479)
XLA Ops:
  0.0 0.5 %collective-permute-start = (s32[384,96]{0,1:T(8,128)}, s32[384,96]{0,1:T(8,128)S(1)}, u32[]{:S(2)}, u32[]{:S(2)}) collective-permute-start(s32[384,96]{0,1:T(8,128)} %param.4), channel_id=1, source_target_pairs={{0,1},{1,0},{2,3},{3,2},{4,5},{5,4},{6,7},{7,6},{8,9},{9,8},{10,11... | collective-permute-start | bytes 442376 | tf_op jit(solution)/shard_map/ppermute | solution.py:205
  0.5 0.1 collective-permute-start.1
  0.5 0.5 %collective-permute-start.2 = (s32[384]{0:T(512)}, s32[384]{0:T(512)S(1)}, u32[]{:S(2)}, u32[]{:S(2)}) collective-permute-start(s32[384]{0:T(512)} %slot_ref.1), channel_id=1, source_target_pairs={{0,1},{1,0},{2,3},{3,2},{4,5},{5,4},{6,7},{7,6},{8,9},{9,8},{10,11... | collective-permute-start | bytes 4616 | tf_op jit(solution)/shard_map/ppermute | solution.py:205
  1.0 0.0 copy-start.1
  1.0 0.9 %copy-done.1 = s32[384,96]{0,1:T(8,128)S(1)} copy-done((s32[384,96]{0,1:T(8,128)S(1)}, s32[384,96]{0,1:T(8,128)}, u32[]{:S(2)}) %copy-start.1) | copy-done | bytes 147480
  1.9 0.0 copy-start.2
  1.9 0.7 %copy-done.2 = s32[384]{0:T(512)S(1)} copy-done((s32[384]{0:T(512)S(1)}, s32[384]{0:T(512)}, u32[]{:S(2)}) %copy-start.2) | copy-done | bytes 1560
  2.6 0.0 copy-start.3
  2.6 0.7 %copy-done.3 = s32[384]{0:T(512)S(1)} copy-done((s32[384]{0:T(512)S(1)}, s32[384]{0:T(512)}, u32[]{:S(2)}) %copy-start.3) | copy-done | bytes 1560
  3.2 0.0 copy-start
  3.3 0.0 collective-permute-done.1.cluster_ref
  3.3 0.0 collective-permute-done.2.slot_ref
  3.3 0.0 collective-permute-done
  3.3 3.7 %collective-permute-start.3 = (bf16[112,768]{1,0:T(8,128)(2,1)S(1)}, bf16[112,768]{1,0:T(8,128)(2,1)S(1)}, u32[]{:S(2)}, u32[]{:S(2)}) collective-permute-start(bf16[112,768]{1,0:T(8,128)(2,1)S(1)} %join.1.packed_ref.refs_0_.own_ref), channel_id=1, source_target_pairs={{0,8},{1,5},{2,10},{3,7},{4,12},{5,1},{6,14},{7,3},{8,0},{9,13},{1... | collective-permute-start | bytes 516104 | tf_op jit(solution)/shard_map/ppermute | solution.py:205
  7.0 0.0 copy-done
  7.0 1.1 %decode_own.1 = (bf16[768,256]{1,0:T(8,128)(2,1)S(1)}, bf16[768,768]{1,0:T(8,128)(2,1)S(1)}) custom-call(bf16[256,768]{1,0:T(8,128)(2,1)S(1)} %copy-done, bf16[112,768]{1,0:T(8,128)(2,1)S(1)} %join.1.packed_ref.refs_0_.own_ref), custom_call_target="tpu_custom_call" | custom-call | flops 1380000000 | tf_op jit(solution)/shard_map/decode_own/pallas_call | solution.py:234
  8.1 2.9 %collective-permute-done.3.refs_2_.direct_ref = bf16[112,768]{1,0:T(8,128)(2,1)S(1)} collective-permute-done((bf16[112,768]{1,0:T(8,128)(2,1)S(1)}, bf16[112,768]{1,0:T(8,128)(2,1)S(1)}, u32[]{:S(2)}, u32[]{:S(2)}) %collective-permute-start.3) | collective-permute-done | bytes 172064 | tf_op jit(solution)/shard_map/ppermute | solution.py:205
  11.1 0.1 collective-permute-start.5
  11.1 2.1 %collective-permute-start.4 = (bf16[112,768]{1,0:T(8,128)(2,1)S(1)}, bf16[112,768]{1,0:T(8,128)(2,1)S(1)}, u32[]{:S(2)}, u32[]{:S(2)}) collective-permute-start(bf16[112,768]{1,0:T(8,128)(2,1)S(1)} %join.1.packed_ref.refs_0_.own_ref), channel_id=1, source_target_pairs={{0,2},{1,7},{2,0},{3,5},{4,6},{5,3},{6,4},{7,1},{8,10},{9,15},{10,... | collective-permute-start | bytes 516104 | tf_op jit(solution)/shard_map/ppermute | solution.py:205
  13.2 1.4 %columns_first.1 = (bf16[768,768]{1,0:T(8,128)(2,1)S(1)}, s32[768,128]{1,0:T(8,128)S(1)}) custom-call(bf16[112,768]{1,0:T(8,128)(2,1)S(1)} %join.1.packed_ref.refs_0_.own_ref, bf16[768,768]{1,0:T(8,128)(2,1)S(1)} %get-tuple-element.17.refs_1_.rows_ref, bf16[112,768]{1,0:T(8,128)(2,1)S(1)} %collective-permute-done.3.refs_2_.direct_ref, ...), custom_call_target="tpu_custom_call" | custom-call | flops 1380000000 | tf_op jit(solution)/shard_map/columns_first/pallas_call | solution.py:243
  14.7 0.0 collective-permute-done.5.passed_ref
  14.7 2.5 %far_first.1 = (bf16[16,768]{1,0:T(8,128)(2,1)S(1)}, bf16[768,768]{1,0:T(8,128)(2,1)S(1)}, f32[1,768]{1,0:T(1,128)S(1)}) custom-call(bf16[112,768]{1,0:T(8,128)(2,1)S(1)} %collective-permute-done.3.refs_2_.direct_ref, bf16[112,768]{1,0:T(8,128)(2,1)S(1)} %collective-permute-done.5.passed_ref, bf16[768,256]{1,0:T(8,128)(2,1)S(1)} %get-tuple-element.20.refs_3_.table_ref, ...), custom_call_target="tpu_custom_call" | custom-call | flops 2300000000 | tf_op jit(solution)/shard_map/far_first/pallas_call | solution.py:250
  17.2 1.2 %collective-permute-done.4.packed_ref = bf16[112,768]{1,0:T(8,128)(2,1)S(1)} collective-permute-done((bf16[112,768]{1,0:T(8,128)(2,1)S(1)}, bf16[112,768]{1,0:T(8,128)(2,1)S(1)}, u32[]{:S(2)}, u32[]{:S(2)}) %collective-permute-start.4) | collective-permute-done | bytes 172064 | tf_op jit(solution)/shard_map/ppermute | solution.py:205
  18.4 2.7 %far_next.1 = (bf16[768,768]{1,0:T(8,128)(2,1)S(1)}, s32[768,128]{1,0:T(8,128)S(1)}, f32[1,768]{1,0:T(1,128)S(1)}) custom-call(bf16[112,768]{1,0:T(8,128)(2,1)S(1)} %collective-permute-done.4.packed_ref, bf16[768,256]{1,0:T(8,128)(2,1)S(1)} %get-tuple-element.20.refs_3_.table_ref, bf16[16,768]{1,0:T(8,128)(2,1)S(1)} %get-tuple-element.23.meta_ref, ...), custom_call_target="tpu_custom_call" | custom-call | flops 2300000000 | tf_op jit(solution)/shard_map/far_next/pallas_call | solution.py:259
  21.1 2.6 %collective-permute-start.6 = (f32[1,768]{1,0:T(1,128)S(1)}, f32[1,768]{1,0:T(1,128)S(1)}, u32[]{:S(2)}, u32[]{:S(2)}) collective-permute-start(f32[1,768]{1,0:T(1,128)S(1)} %get-tuple-element.28), channel_id=1, source_target_pairs={{0,8},{1,9},{2,10},{3,11},{4,12},{5,13},{6,14},{7,15},{8,0},{9,1},... | collective-permute-start | bytes 9224 | tf_op jit(solution)/shard_map/ppermute | solution.py:205
  23.8 2.1 %near.1 = f32[1,768]{1,0:T(1,128)S(1)} custom-call(bf16[112,768]{1,0:T(8,128)(2,1)S(1)} %join.1.packed_ref.refs_0_.own_ref, bf16[768,768]{1,0:T(8,128)(2,1)S(1)} %get-tuple-element.17.refs_1_.rows_ref, bf16[768,768]{1,0:T(8,128)(2,1)S(1)} %get-tuple-element.21.columns_ref.refs_0_, s32[768,128]{1,0:T(8,128)S(1)} %get-tuple-element.22.key_ref.refs_1_, ...), custom_call_target="tpu_custom_call" | custom-call | flops 2300000000 | tf_op jit(solution)/shard_map/near/pallas_call | solution.py:267
  25.9 0.0 collective-permute-done.6
  26.0 0.6 %collective-permute-start.7 = (f32[1,384]{1,0:T(1,128)S(1)}, f32[1,384]{1,0:T(1,128)S(1)}, u32[]{:S(2)}, u32[]{:S(2)}) collective-permute-start(f32[1,384]{1,0:T(1,128)S(1)} %broadcast_select_fusion), channel_id=1, source_target_pairs={{0,1},{1,0},{2,3},{3,2},{4,5},{5,4},{6,7},{7,6},{8,9},{9,8},{10,11... | collective-permute-start | bytes 4616 | tf_op jit(solution)/shard_map/ppermute | solution.py:205
  26.6 0.8 %collective-permute-done.7 = f32[1,384]{1,0:T(1,128)S(1)} collective-permute-done((f32[1,384]{1,0:T(1,128)S(1)}, f32[1,384]{1,0:T(1,128)S(1)}, u32[]{:S(2)}, u32[]{:S(2)}) %collective-permute-start.7) | collective-permute-done | bytes 1568 | tf_op jit(solution)/shard_map/ppermute | solution.py:205
  27.4 0.6 %fusion.1 = f32[384]{0:T(512)} fusion(f32[1,384]{1,0:T(1,128)S(1)} %collective-permute-done.7, pred[]{:T(512)S(6)} %eq.4, f32[1,768]{1,0:T(1,128)S(1)} %max.6), kind=kLoop, calls=%fused_computation.3 | loop fusion | flops 768 | bytes 6145 | tf_op jit(solution)/shard_map/max | solution.py:274
  (4 shorter events, 0.1 us)
Async XLA Ops:
  0.0 3.3 %collective-permute-start = (s32[384,96]{0,1:T(8,128)}, s32[384,96]{0,1:T(8,128)S(1)}, u32[]{:S(2)}, u32[]{:S(2)}) collective-permute-start(s32[384,96]{0,1:T(8,128)} %param.4), channel_id=1, source_target_pairs={{0,1},{1,0},{2,3},{3,2},{4,5},{5,4},{6,7},{7,6},{8,9},{9,8},{10,11... | collective-permute-start | bytes 442376 | tf_op jit(solution)/shard_map/ppermute | solution.py:205
  0.5 2.8 %collective-permute-start.1 = (s32[384]{0:T(512)}, s32[384]{0:T(512)S(1)}, u32[]{:S(2)}, u32[]{:S(2)}) collective-permute-start(s32[384]{0:T(512)} %cluster_ref.1), channel_id=1, source_target_pairs={{0,1},{1,0},{2,3},{3,2},{4,5},{5,4},{6,7},{7,6},{8,9},{9,8},{10,11... | collective-permute-start | bytes 4616 | tf_op jit(solution)/shard_map/ppermute | solution.py:205
  0.5 2.8 %collective-permute-start.2 = (s32[384]{0:T(512)}, s32[384]{0:T(512)S(1)}, u32[]{:S(2)}, u32[]{:S(2)}) collective-permute-start(s32[384]{0:T(512)} %slot_ref.1), channel_id=1, source_target_pairs={{0,1},{1,0},{2,3},{3,2},{4,5},{5,4},{6,7},{7,6},{8,9},{9,8},{10,11... | collective-permute-start | bytes 4616 | tf_op jit(solution)/shard_map/ppermute | solution.py:205
  1.0 0.9 %copy-start.1 = (s32[384,96]{0,1:T(8,128)S(1)}, s32[384,96]{0,1:T(8,128)}, u32[]{:S(2)}) copy-start(s32[384,96]{0,1:T(8,128)} %param.4) | copy-start | bytes 442372
  1.9 0.7 %copy-start.2 = (s32[384]{0:T(512)S(1)}, s32[384]{0:T(512)}, u32[]{:S(2)}) copy-start(s32[384]{0:T(512)} %cluster_ref.1) | copy-start | bytes 4612
  2.6 0.7 %copy-start.3 = (s32[384]{0:T(512)S(1)}, s32[384]{0:T(512)}, u32[]{:S(2)}) copy-start(s32[384]{0:T(512)} %slot_ref.1) | copy-start | bytes 4612
  3.2 3.8 %copy-start = (bf16[256,768]{1,0:T(8,128)(2,1)S(1)}, bf16[256,768]{1,0:T(8,128)(2,1)}, u32[]{:S(2)}) copy-start(bf16[256,768]{1,0:T(8,128)(2,1)} %codebook_ref.1) | copy-start | bytes 1179652
  3.3 7.7 %collective-permute-start.3 = (bf16[112,768]{1,0:T(8,128)(2,1)S(1)}, bf16[112,768]{1,0:T(8,128)(2,1)S(1)}, u32[]{:S(2)}, u32[]{:S(2)}) collective-permute-start(bf16[112,768]{1,0:T(8,128)(2,1)S(1)} %join.1.packed_ref.refs_0_.own_ref), channel_id=1, source_target_pairs={{0,8},{1,5},{2,10},{3,7},{4,12},{5,1},{6,14},{7,3},{8,0},{9,13},{1... | collective-permute-start | bytes 516104 | tf_op jit(solution)/shard_map/ppermute | solution.py:205
  11.1 3.6 %collective-permute-start.5 = (bf16[112,768]{1,0:T(8,128)(2,1)S(1)}, bf16[112,768]{1,0:T(8,128)(2,1)S(1)}, u32[]{:S(2)}, u32[]{:S(2)}) collective-permute-start(bf16[112,768]{1,0:T(8,128)(2,1)S(1)} %collective-permute-done.3.refs_2_.direct_ref), channel_id=1, source_target_pairs={{0,1},{1,0},{2,3},{3,2},{4,5},{5,4},{6,7},{7,6},{8,9},{9,8},{10,11... | collective-permute-start | bytes 516104 | tf_op jit(solution)/shard_map/ppermute | solution.py:205
  11.1 7.3 %collective-permute-start.4 = (bf16[112,768]{1,0:T(8,128)(2,1)S(1)}, bf16[112,768]{1,0:T(8,128)(2,1)S(1)}, u32[]{:S(2)}, u32[]{:S(2)}) collective-permute-start(bf16[112,768]{1,0:T(8,128)(2,1)S(1)} %join.1.packed_ref.refs_0_.own_ref), channel_id=1, source_target_pairs={{0,2},{1,7},{2,0},{3,5},{4,6},{5,3},{6,4},{7,1},{8,10},{9,15},{10,... | collective-permute-start | bytes 516104 | tf_op jit(solution)/shard_map/ppermute | solution.py:205
  21.1 4.8 %collective-permute-start.6 = (f32[1,768]{1,0:T(1,128)S(1)}, f32[1,768]{1,0:T(1,128)S(1)}, u32[]{:S(2)}, u32[]{:S(2)}) collective-permute-start(f32[1,768]{1,0:T(1,128)S(1)} %get-tuple-element.28), channel_id=1, source_target_pairs={{0,8},{1,9},{2,10},{3,11},{4,12},{5,13},{6,14},{7,15},{8,0},{9,1},... | collective-permute-start | bytes 9224 | tf_op jit(solution)/shard_map/ppermute | solution.py:205
  26.0 1.5 %collective-permute-start.7 = (f32[1,384]{1,0:T(1,128)S(1)}, f32[1,384]{1,0:T(1,128)S(1)}, u32[]{:S(2)}, u32[]{:S(2)}) collective-permute-start(f32[1,384]{1,0:T(1,128)S(1)} %broadcast_select_fusion), channel_id=1, source_target_pairs={{0,1},{1,0},{2,3},{3,2},{4,5},{5,4},{6,7},{7,6},{8,9},{9,8},{10,11... | collective-permute-start | bytes 4616 | tf_op jit(solution)/shard_map/ppermute | solution.py:205

commit v3 on v2

v3 whole, which is shorter than its diff:
```python
import functools

import jax
import jax.numpy as jnp
from jax import lax
from jax.experimental import pallas as pl
from jax.experimental.pallas import tpu as pltpu
from jax.sharding import PartitionSpec as P

LANES = 128
META_ROWS = 8
BLOCK_SUBS = 16
STEP_ROWS = 768
STEP_LANES = 256
AXES = ("group", "tile")
GATHER = lax.GatherDimensionNumbers(
    offset_dims=(),
    collapsed_slice_dims=(1,),
    start_index_map=(1,),
    operand_batching_dims=(0,),
    start_indices_batching_dims=(0,),
)


def core_index():
    return lax.rem(lax.axis_index("tile"), 2)


def gather_lanes(table, index):
    return lax.gather(
        table, index[..., None], GATHER, slice_sizes=(1, 1), mode=lax.GatherScatterMode.PROMISE_IN_BOUNDS
    )


def integers(values):
    return values.astype(jnp.float32).astype(jnp.int32)


def read_keys(meta):
    meta = integers(meta)
    key = ((meta[3:4] * 256 + meta[2:3]) * 256 + meta[1:2]) * 256 + meta[0:1]
    return key, key - (meta[5:6] * 256 + meta[4:5])


def spread_keys(key, out_ref):
    for c in range(key.shape[1] // LANES):
        lanes = slice(c * LANES, (c + 1) * LANES)
        out_ref[lanes, :] = jnp.broadcast_to(key[:, lanes], (LANES, LANES)).T


def make_table(codebook_ref, table_ref, wide_ref, sub_dim):
    features = table_ref.shape[0]
    wide = codebook_ref[...].astype(jnp.float32).T
    for half in range(wide.shape[1] // LANES):
        lanes = slice(half * LANES, (half + 1) * LANES)
        wide_ref[...] = wide[:, lanes]
        for first in range(0, features, BLOCK_SUBS * sub_dim):
            for e in range(sub_dim):
                row = first + e * BLOCK_SUBS
                strided = wide_ref[pl.ds(first + e, BLOCK_SUBS, stride=sub_dim), :]
                table_ref[row : row + BLOCK_SUBS, lanes] = strided.astype(jnp.bfloat16)


def decode(codes, table_ref, exact_ref, out_ref, chunks=None):
    features = table_ref.shape[0]
    subs, rows = codes.shape
    sub_dim = features // subs
    for c in range(rows // LANES) if chunks is None else chunks:
        lanes = slice(c * LANES, (c + 1) * LANES)
        total = jnp.zeros((8, LANES), jnp.float32)
        for block in range(subs // BLOCK_SUBS):
            chosen = integers(codes[block * BLOCK_SUBS : (block + 1) * BLOCK_SUBS, lanes]).astype(jnp.int16)
            index = chosen & (LANES - 1)
            in_low = chosen < LANES
            for e in range(sub_dim):
                row = (block * sub_dim + e) * BLOCK_SUBS
                table = table_ref[row : row + BLOCK_SUBS, :]
                low, high = gather_lanes(table[:, :LANES], index), gather_lanes(table[:, LANES:], index)
                exact = jnp.where(in_low, low, high)
                exact_ref[row : row + BLOCK_SUBS, lanes] = exact
                square = exact.astype(jnp.float32)
                square = square * square
                total = total + square[:8] + square[8:]
        inverse = lax.rsqrt(jnp.sum(total, axis=0, keepdims=True) + 1e-06)
        inverse = jnp.broadcast_to(inverse, (BLOCK_SUBS, LANES))
        for row in range(0, features, BLOCK_SUBS):
            exact = exact_ref[row : row + BLOCK_SUBS, lanes].astype(jnp.float32)
            out_ref[row : row + BLOCK_SUBS, lanes] = (exact * inverse).astype(jnp.bfloat16)


def meta_rows(cluster, slot, group_slots, groups):
    local = slot
    for g in range(1, groups):
        local = local - jnp.where(slot >= g * group_slots, group_slots, 0)
    key = cluster * group_slots + local
    digits = [key & 255, (key >> 8) & 255, (key >> 16) & 255, key >> 24, local & 255, local >> 8]
    row = lax.broadcasted_iota(jnp.int32, (META_ROWS, key.shape[1]), 0)
    meta = jnp.zeros(row.shape, jnp.int32)
    for d, digit in enumerate(digits):
        meta = jnp.where(row == d, digit, meta)
    return meta.astype(jnp.float32).astype(jnp.bfloat16)


def pack(codes, cluster, slot, group_slots, groups):
    subs, rows = codes.shape
    meta = meta_rows(cluster.reshape(1, rows), slot.reshape(1, rows), group_slots, groups)
    return codes.astype(jnp.float32).astype(jnp.bfloat16), meta


def pack_kernel(group_slots, groups, *refs):
    sources, out_ref, buffers, sems = refs[:3], refs[3], refs[4:7], refs[7]
    copies = [
        pltpu.make_async_copy(source, buffer, sems.at[k]) for k, (source, buffer) in enumerate(zip(sources, buffers))
    ]
    for copy in copies:
        copy.start()
    for copy in copies:
        copy.wait()
    codes, meta = pack(*(buffer[...] for buffer in buffers), group_slots, groups)
    out_ref[: codes.shape[0], :] = codes
    out_ref[codes.shape[0] :, :] = meta


def join_kernel(group_slots, groups, packed_ref, codes_ref, cluster_ref, slot_ref, out_ref):
    subs, rows = codes_ref.shape
    codes, meta = pack(codes_ref[...], cluster_ref[...], slot_ref[...], group_slots, groups)
    for half in range(2):
        mine = core_index() == half
        lanes = slice(half * rows, (half + 1) * rows)
        out_ref[:subs, lanes] = jnp.where(mine, packed_ref[:subs, :], codes)
        out_ref[subs:, lanes] = jnp.where(mine, packed_ref[subs:, :], meta)


def own_kernel(codebook_ref, packed_ref, table_ref, out_ref, wide_ref, exact_ref):
    subs = packed_ref.shape[0] - META_ROWS
    make_table(codebook_ref, table_ref, wide_ref, codebook_ref.shape[1] // subs)
    rows_kernel(packed_ref, table_ref, out_ref, exact_ref)


def rows_kernel(packed_ref, table_ref, out_ref, exact_ref):
    features = table_ref.shape[0]
    subs = packed_ref.shape[0] - META_ROWS
    decode(packed_ref[:subs, :], table_ref, exact_ref, out_ref)
    out_ref[features:, :] = packed_ref[subs:, :]


def columns_kernel(packed_ref, table_ref, columns_ref, key_ref, exact_ref, unit_ref):
    subs = packed_ref.shape[0] - META_ROWS
    decode(packed_ref[:subs, :], table_ref, exact_ref, unit_ref)
    columns_ref[...] = unit_ref[...].T
    spread_keys(read_keys(packed_ref[subs:, :])[0], key_ref)


def last_kernel(own_ref, packed_ref, table_ref, rows_ref, columns_ref, key_ref, exact_ref):
    features = columns_ref.shape[1]
    rows_kernel(packed_ref, table_ref, rows_ref, exact_ref)
    core0 = core_index() == 0
    columns_ref[...] = jnp.where(core0, own_ref[:features, :], rows_ref[:features, :]).T
    spread_keys(read_keys(jnp.where(core0, own_ref[features:, :], rows_ref[features:, :]))[0], key_ref)


def masked_max(columns_ref, key_ref, span, rows, key, base, best):
    scores = jnp.dot(columns_ref[span, :], rows, preferred_element_type=jnp.float32)
    keys = jnp.concatenate([key_ref[span, :]] * (scores.shape[1] // LANES), axis=1)
    scores = jnp.where((keys < key) & (keys >= base), scores, -1.0)
    return jnp.maximum(best, jnp.max(scores.reshape(scores.shape[0] // 8, 8, scores.shape[1]), axis=0))


def lane_steps(ref):
    return [slice(first, first + STEP_LANES) for first in range(0, ref.shape[1], STEP_LANES)]


def score(rows_ref, pairs, best_ref):
    features = pairs[0][0].shape[1]
    key, base = read_keys(rows_ref[features:, :])
    for lanes in lane_steps(rows_ref):
        best = jnp.full((8, STEP_LANES), -1.0, jnp.float32)
        for columns_ref, key_ref in pairs:
            for first in range(0, columns_ref.shape[0], STEP_ROWS):
                best = masked_max(
                    columns_ref,
                    key_ref,
                    slice(first, first + STEP_ROWS),
                    rows_ref[:features, lanes],
                    key[:, lanes],
                    base[:, lanes],
                    best,
                )
        best_ref[:, lanes] = jnp.max(best, axis=0, keepdims=True)


def far_kernel(direct_ref, passed_ref, table_ref, *refs):
    *columns, best_ref, rows_ref, exact_ref = refs
    core = core_index()

    @pl.when(core == 0)
    def _():
        rows_ref[...] = direct_ref[...]

    @pl.when(core != 0)
    def _():
        rows_kernel(passed_ref, table_ref, rows_ref, exact_ref)

    score(rows_ref, list(zip(columns[::2], columns[1::2])), best_ref)


def near_kernel(rows_ref, *refs):
    *columns, best_ref = refs
    score(rows_ref, list(zip(columns[::2], columns[1::2])), best_ref)


def call(kernel, microseconds, name, out_shape, scratch=(), in_specs=None):
    return pl.pallas_call(
        kernel,
        **({} if in_specs is None else {"in_specs": [in_specs] * 3}),
        out_shape=out_shape,
        scratch_shapes=scratch,
        compiler_params=pltpu.CompilerParams(vmem_limit_bytes=12 * 1024 * 1024),
        cost_estimate=pl.CostEstimate(flops=int(microseconds * 1.15e9), bytes_accessed=0, transcendentals=0),
        name=name,
    )


def body(product_codes, member_cluster, member_slot, codebook):
    row_count, subs = product_codes.shape
    code_count, features = codebook.shape
    groups = lax.axis_size("group")
    tiles = lax.axis_size("tile")
    devices = groups * tiles
    pair_rows = 2 * row_count
    group_slots = tiles * 2 * row_count
    packed_rows = subs + META_ROWS
    core = core_index()

    def exchange(value, offset_core0, offset_core1):
        pairs = [(i, i ^ (offset_core0 if i % 2 == 0 else offset_core1)) for i in range(devices)]
        return lax.ppermute(value, AXES, pairs)

    far = (groups // 2) * tiles
    chips = [dz * tiles + dx * 2 for dz in range(groups // 2) for dx in range(tiles // 2)]
    half = len(chips) // 2
    first_chips, second_chips = chips[:half], chips[half:]

    shape = jax.ShapeDtypeStruct
    bf16 = jnp.bfloat16
    exact_scratch = pltpu.VMEM((features, pair_rows), bf16)
    rows_shape = shape((features + META_ROWS, pair_rows), bf16)
    best_shape = shape((1, pair_rows), jnp.float32)

    mine = (product_codes, member_cluster, member_slot)
    other_codes, other_cluster, other_slot = (exchange(value, 1, 1) for value in mine)
    packed = call(
        functools.partial(pack_kernel, group_slots, groups),
        0.3,
        "pack",
        shape((packed_rows, row_count), bf16),
        [pltpu.VMEM((subs, row_count), jnp.int32)]
        + [pltpu.VMEM((row_count,), jnp.int32)] * 2
        + [pltpu.SemaphoreType.DMA((3,))],
        pl.BlockSpec(memory_space=pltpu.MemorySpace.HBM),
    )(*(pltpu.with_memory_space_constraint(v, pltpu.MemorySpace.HBM) for v in (product_codes.T, *mine[1:])))
    own = call(
        functools.partial(join_kernel, group_slots, groups),
        0.3,
        "join",
        shape((packed_rows, pair_rows), bf16),
    )(packed, other_codes.T, other_cluster, other_slot)
    arrived = [exchange(own, first_chips[k] or far, second_chips[k - 1]) for k in [*range(1, half), 0]]

    table, own_rows = call(
        own_kernel,
        1.2,
        "decode_own",
        (shape((features, code_count), bf16), rows_shape),
        [pltpu.VMEM((features, LANES), jnp.float32), exact_scratch],
    )(codebook, own)
    column_shapes = (shape((pair_rows, features), bf16), shape((pair_rows, LANES), jnp.int32))
    columns = []
    for latest in arrived[:-1]:
        latest, table, own_rows = lax.optimization_barrier((latest, table, own_rows))
        columns.append(
            call(columns_kernel, 1.2, "columns", column_shapes, [exact_scratch, exact_scratch])(latest, table)
        )
    last, table, columns = lax.optimization_barrier((arrived[-1], table, columns))
    passed = exchange(last, 1, 1)
    last_rows, *last_columns = call(last_kernel, 1.4, "last", (rows_shape, *column_shapes), [exact_scratch])(
        own_rows, last, table
    )
    columns.append(last_columns)
    rows_scratch = pltpu.VMEM(rows_shape.shape, bf16)
    far_best, near_best = None, None
    for k in range(0, half, 2):
        batch = [array for pair in columns[k : k + 2] for array in pair]
        far_part = call(far_kernel, 2.7, "score_far", best_shape, [rows_scratch, exact_scratch])(
            last_rows, passed, table, *batch
        )
        near_part = call(near_kernel, 2.0, "score_near", best_shape)(own_rows, *batch)
        far_best = far_part if far_best is None else jnp.maximum(far_best, far_part)
        near_best = near_part if near_best is None else jnp.maximum(near_best, near_part)

    returned = exchange(far_best, far, far)
    total = jnp.maximum(near_best, returned)
    first, second = total[:, :row_count], total[:, row_count:]
    keep = jnp.where(core == 0, first, second)
    other = exchange(jnp.where(core == 0, second, first), 1, 1)
    return jnp.maximum(keep, other).reshape(row_count)


def solution(mesh):
    placed = (
        P(("parts", "group", "tile"), None),
        P(("parts", "group", "tile")),
        P(("parts", "group", "tile")),
        P(),
    )
    return jax.shard_map(
        body, mesh=mesh, in_specs=placed, out_specs=P(("parts", "group", "tile")), check_vma=False
    )
```

time: 28.2 us -> 23.1 us (0.82)
  local copies, waits for them, and re-layouts: 2.28 us -> 0.01 us
  waiting for transfers between devices: 4.99 us -> 2.73 us
  Pallas kernels: 9.99 us -> 9.32 us
    unnamed x8 -> x2, local copies, waits for them, and re-layouts: 2.28 us -> 0.01 us
    ppermute x8, waiting for transfers between devices: 4.99 us -> 2.73 us  [exchange(): return lax.ppermute(value, AXES, pairs)]
    pallas_call x4, Pallas kernels: 8.81 us -> 7.15 us  [the longest x1 2.23 us: body(): call(far_kernel, 2.7, 'score_far', best_shape, [rows_scratch, exact_scrat...]
    pallas_call x1, Pallas kernels: 0.02 us -> 1.01 us  [body(): call(functools.partial(pack_kernel, group_slots, groups), 0.3, 'pack', sh...]
  transfers between devices with their start and end apart: 8 -> 8, of which waited for: 3 -> 3; matrix products, arithmetic and copies ran while one was open for 0% -> 0% of each run, Pallas kernels for 26% -> 31%
where the time goes in v3:
time: 23.1 us; the launch traced here: 22.7 us
  starting transfers between devices  9.94 us (43%)
  Pallas kernels  9.32 us (40%)
  waiting for transfers between devices  2.73 us (12%)
  other arithmetic  0.61 us (3%)
    ppermute x8, starting transfers between devices, exchange(): return lax.ppermute(value, AXES, pairs)  9.94 us
    ppermute x8, waiting for transfers between devices, exchange(): return lax.ppermute(value, AXES, pairs)  2.73 us
    pallas_call x1, Pallas kernels, body(): call(far_kernel, 2.7, 'score_far', best_shape, [rows_scratch, exact_scrat...  2.23 us
    pallas_call x1, Pallas kernels, body(): call(near_kernel, 2.0, 'score_near', best_shape)(own_rows, *batch)  2.15 us
    pallas_call x1, Pallas kernels, body(): call(last_kernel, 1.4, 'last', (rows_shape, *column_shapes), [exact_scrat...  1.43 us
    pallas_call x1, Pallas kernels, body(): call(columns_kernel, 1.2, 'columns', column_shapes, [exact_scratch, exact...  1.34 us
    pallas_call x1, Pallas kernels, body(): call(own_kernel, 1.2, 'decode_own', (shape((features, code_count), bf16),...  1.12 us
    pallas_call x1, Pallas kernels, body(): call(functools.partial(pack_kernel, group_slots, groups), 0.3, 'pack', sh...  1.01 us
  transfers between devices with their start and end apart: 8, of which 3 were waited for; matrix products, arithmetic and copies ran while one was open for 0% of the time, Pallas kernels for 31%

profile of v3, /device:TPU:0, one launch (start us, length us, event | category | flops | bytes accessed | tf_op | source)
XLA Modules:
  0.0 22.7 jit_solution(13989940392463157472)
XLA Ops:
  0.0 0.5 %collective-permute-start = (s32[384,96]{0,1:T(8,128)}, s32[384,96]{0,1:T(8,128)S(1)}, u32[]{:S(2)}, u32[]{:S(2)}) collective-permute-start(s32[384,96]{0,1:T(8,128)} %param.4), channel_id=1, source_target_pairs={{0,1},{1,0},{2,3},{3,2},{4,5},{5,4},{6,7},{7,6},{8,9},{9,8},{10,11... | collective-permute-start | bytes 442376 | tf_op jit(solution)/shard_map/ppermute | solution.py:237
  0.5 0.1 collective-permute-start.1
  0.5 0.5 %collective-permute-start.2 = (s32[384]{0:T(512)}, s32[384]{0:T(512)S(1)}, u32[]{:S(2)}, u32[]{:S(2)}) collective-permute-start(s32[384]{0:T(512)} %refs_2_.1), channel_id=1, source_target_pairs={{0,1},{1,0},{2,3},{3,2},{4,5},{5,4},{6,7},{7,6},{8,9},{9,8},{10,11... | collective-permute-start | bytes 4616 | tf_op jit(solution)/shard_map/ppermute | solution.py:237
  1.0 0.0 copy-start
  1.0 1.0 %pack.1.packed_ref = bf16[104,384]{1,0:T(8,128)(2,1)S(1)} custom-call(s32[96,384]{1,0:T(8,128)} %bitcast.3, s32[384]{0:T(512)} %refs_1_.1, s32[384]{0:T(512)} %refs_2_.1), custom_call_target="tpu_custom_call" | custom-call | flops 345000000 | tf_op jit(solution)/shard_map/pack/pallas_call | solution.py:252
  2.0 0.0 collective-permute-done.1.cluster_ref
  2.0 0.0 collective-permute-done.2.slot_ref
  2.0 0.0 collective-permute-done
  2.1 2.9 %collective-permute-start.3 = (bf16[104,768]{1,0:T(8,128)(2,1)S(1)}, bf16[104,768]{1,0:T(8,128)(2,1)S(1)}, u32[]{:S(2)}, u32[]{:S(2)}) collective-permute-start(bf16[104,768]{1,0:T(8,128)(2,1)S(1)} %join.1.packed_ref), channel_id=1, source_target_pairs={{0,2},{1,5},{2,0},{3,7},{4,6},{5,1},{6,4},{7,3},{8,10},{9,13},{10,... | collective-permute-start | bytes 479240 | tf_op jit(solution)/shard_map/ppermute | solution.py:237
  4.9 2.6 %collective-permute-start.4 = (bf16[104,768]{1,0:T(8,128)(2,1)S(1)}, bf16[104,768]{1,0:T(8,128)(2,1)S(1)}, u32[]{:S(2)}, u32[]{:S(2)}) collective-permute-start(bf16[104,768]{1,0:T(8,128)(2,1)S(1)} %join.1.packed_ref), channel_id=1, source_target_pairs={{0,8},{1,7},{2,10},{3,5},{4,12},{5,3},{6,14},{7,1},{8,0},{9,15},{1... | collective-permute-start | bytes 479240 | tf_op jit(solution)/shard_map/ppermute | solution.py:237
  7.5 0.0 copy-done
  7.5 1.1 %decode_own.1 = (bf16[768,256]{1,0:T(8,128)(2,1)S(1)}, bf16[776,768]{1,0:T(8,128)(2,1)S(1)}) custom-call(bf16[256,768]{1,0:T(8,128)(2,1)S(1)} %copy-done, bf16[104,768]{1,0:T(8,128)(2,1)S(1)} %join.1.packed_ref), custom_call_target="tpu_custom_call" | custom-call | flops 1380000000 | tf_op jit(solution)/shard_map/decode_own/pallas_call | solution.py:270
  8.6 0.2 collective-permute-done.3.packed_ref
  8.8 1.3 %columns.1 = (bf16[768,768]{1,0:T(8,128)(2,1)S(1)}, s32[768,128]{1,0:T(8,128)S(1)}) custom-call(bf16[104,768]{1,0:T(8,128)(2,1)S(1)} %collective-permute-done.3.packed_ref, bf16[768,256]{1,0:T(8,128)(2,1)S(1)} %get-tuple-element.29.table_ref), custom_call_target="tpu_custom_call" | custom-call | flops 1380000000 | tf_op jit(solution)/shard_map/columns/pallas_call | solution.py:282
  10.1 1.7 %collective-permute-done.4.packed_ref = bf16[104,768]{1,0:T(8,128)(2,1)S(1)} collective-permute-done((bf16[104,768]{1,0:T(8,128)(2,1)S(1)}, bf16[104,768]{1,0:T(8,128)(2,1)S(1)}, u32[]{:S(2)}, u32[]{:S(2)}) %collective-permute-start.4) | collective-permute-done | bytes 159776 | tf_op jit(solution)/shard_map/ppermute | solution.py:237
  11.9 0.2 collective-permute-start.5
  12.1 1.4 %last.1 = (bf16[776,768]{1,0:T(8,128)(2,1)S(1)}, bf16[768,768]{1,0:T(8,128)(2,1)S(1)}, s32[768,128]{1,0:T(8,128)S(1)}) custom-call(bf16[776,768]{1,0:T(8,128)(2,1)S(1)} %get-tuple-element.21.own_ref.rows_ref, bf16[104,768]{1,0:T(8,128)(2,1)S(1)} %collective-permute-done.4.packed_ref, bf16[768,256]{1,0:T(8,128)(2,1)S(1)} %get-tuple-element.29.table_ref), custom_call_target="tpu_custom_call" | custom-call | flops 1610000000 | tf_op jit(solution)/shard_map/last/pallas_call | solution.py:286
  13.5 0.0 collective-permute-done.5.passed_ref
  13.6 2.2 %score_far.1 = f32[1,768]{1,0:T(1,128)S(1)} custom-call(bf16[776,768]{1,0:T(8,128)(2,1)S(1)} %get-tuple-element.32.direct_ref, bf16[104,768]{1,0:T(8,128)(2,1)S(1)} %collective-permute-done.5.passed_ref, bf16[768,256]{1,0:T(8,128)(2,1)S(1)} %get-tuple-element.29.table_ref, bf16[768,768]{1,0:T(8,128)(2,1)S(1)} %get-tuple-element.26.refs_0_, ...), custom_call_target="tpu_custom_call" | custom-call | flops 3104999936 | tf_op jit(solution)/shard_map/score_far/pallas_call | solution.py:294
  15.8 2.7 %collective-permute-start.6 = (f32[1,768]{1,0:T(1,128)S(1)}, f32[1,768]{1,0:T(1,128)S(1)}, u32[]{:S(2)}, u32[]{:S(2)}) collective-permute-start(f32[1,768]{1,0:T(1,128)S(1)} %score_far.1), channel_id=1, source_target_pairs={{0,8},{1,9},{2,10},{3,11},{4,12},{5,13},{6,14},{7,15},{8,0},{9,1},... | collective-permute-start | bytes 9224 | tf_op jit(solution)/shard_map/ppermute | solution.py:237
  18.5 2.2 %score_near.1 = f32[1,768]{1,0:T(1,128)S(1)} custom-call(bf16[776,768]{1,0:T(8,128)(2,1)S(1)} %get-tuple-element.21.own_ref.rows_ref, bf16[768,768]{1,0:T(8,128)(2,1)S(1)} %get-tuple-element.26.refs_0_, s32[768,128]{1,0:T(8,128)S(1)} %get-tuple-element.27.refs_1_, bf16[768,768]{1,0:T(8,128)(2,1)S(1)} %get-tuple-element.30.refs_2_, ...), custom_call_target="tpu_custom_call" | custom-call | flops 2300000000 | tf_op jit(solution)/shard_map/score_near/pallas_call | solution.py:297
  20.6 0.0 collective-permute-done.6
  20.6 0.7 %collective-permute-start.7 = (f32[1,384]{1,0:T(1,128)S(1)}, f32[1,384]{1,0:T(1,128)S(1)}, u32[]{:S(2)}, u32[]{:S(2)}) collective-permute-start(f32[1,384]{1,0:T(1,128)S(1)} %broadcast_select_fusion), channel_id=1, source_target_pairs={{0,1},{1,0},{2,3},{3,2},{4,5},{5,4},{6,7},{7,6},{8,9},{9,8},{10,11... | collective-permute-start | bytes 4616 | tf_op jit(solution)/shard_map/ppermute | solution.py:237
  21.3 0.8 %collective-permute-done.7 = f32[1,384]{1,0:T(1,128)S(1)} collective-permute-done((f32[1,384]{1,0:T(1,128)S(1)}, f32[1,384]{1,0:T(1,128)S(1)}, u32[]{:S(2)}, u32[]{:S(2)}) %collective-permute-start.7) | collective-permute-done | bytes 1568 | tf_op jit(solution)/shard_map/ppermute | solution.py:237
  22.1 0.6 %fusion.1 = f32[384]{0:T(512)} fusion(f32[1,384]{1,0:T(1,128)S(1)} %collective-permute-done.7, pred[]{:T(512)S(6)} %eq.4, f32[1,768]{1,0:T(1,128)S(1)} %max.6), kind=kLoop, calls=%fused_computation.3 | loop fusion | flops 768 | bytes 6145 | tf_op jit(solution)/shard_map/max | solution.py:306
  (3 shorter events, 0.0 us)
Async XLA Ops:
  0.0 2.0 %collective-permute-start = (s32[384,96]{0,1:T(8,128)}, s32[384,96]{0,1:T(8,128)S(1)}, u32[]{:S(2)}, u32[]{:S(2)}) collective-permute-start(s32[384,96]{0,1:T(8,128)} %param.4), channel_id=1, source_target_pairs={{0,1},{1,0},{2,3},{3,2},{4,5},{5,4},{6,7},{7,6},{8,9},{9,8},{10,11... | collective-permute-start | bytes 442376 | tf_op jit(solution)/shard_map/ppermute | solution.py:237
  0.5 1.5 %collective-permute-start.1 = (s32[384]{0:T(512)}, s32[384]{0:T(512)S(1)}, u32[]{:S(2)}, u32[]{:S(2)}) collective-permute-start(s32[384]{0:T(512)} %refs_1_.1), channel_id=1, source_target_pairs={{0,1},{1,0},{2,3},{3,2},{4,5},{5,4},{6,7},{7,6},{8,9},{9,8},{10,11... | collective-permute-start | bytes 4616 | tf_op jit(solution)/shard_map/ppermute | solution.py:237
  0.5 1.5 %collective-permute-start.2 = (s32[384]{0:T(512)}, s32[384]{0:T(512)S(1)}, u32[]{:S(2)}, u32[]{:S(2)}) collective-permute-start(s32[384]{0:T(512)} %refs_2_.1), channel_id=1, source_target_pairs={{0,1},{1,0},{2,3},{3,2},{4,5},{5,4},{6,7},{7,6},{8,9},{9,8},{10,11... | collective-permute-start | bytes 4616 | tf_op jit(solution)/shard_map/ppermute | solution.py:237
  1.0 6.6 %copy-start = (bf16[256,768]{1,0:T(8,128)(2,1)S(1)}, bf16[256,768]{1,0:T(8,128)(2,1)}, u32[]{:S(2)}) copy-start(bf16[256,768]{1,0:T(8,128)(2,1)} %codebook_ref.1) | copy-start | bytes 1179652
  2.1 6.7 %collective-permute-start.3 = (bf16[104,768]{1,0:T(8,128)(2,1)S(1)}, bf16[104,768]{1,0:T(8,128)(2,1)S(1)}, u32[]{:S(2)}, u32[]{:S(2)}) collective-permute-start(bf16[104,768]{1,0:T(8,128)(2,1)S(1)} %join.1.packed_ref), channel_id=1, source_target_pairs={{0,2},{1,5},{2,0},{3,7},{4,6},{5,1},{6,4},{7,3},{8,10},{9,13},{10,... | collective-permute-start | bytes 479240 | tf_op jit(solution)/shard_map/ppermute | solution.py:237
  4.9 7.0 %collective-permute-start.4 = (bf16[104,768]{1,0:T(8,128)(2,1)S(1)}, bf16[104,768]{1,0:T(8,128)(2,1)S(1)}, u32[]{:S(2)}, u32[]{:S(2)}) collective-permute-start(bf16[104,768]{1,0:T(8,128)(2,1)S(1)} %join.1.packed_ref), channel_id=1, source_target_pairs={{0,8},{1,7},{2,10},{3,5},{4,12},{5,3},{6,14},{7,1},{8,0},{9,15},{1... | collective-permute-start | bytes 479240 | tf_op jit(solution)/shard_map/ppermute | solution.py:237
  11.9 1.7 %collective-permute-start.5 = (bf16[104,768]{1,0:T(8,128)(2,1)S(1)}, bf16[104,768]{1,0:T(8,128)(2,1)S(1)}, u32[]{:S(2)}, u32[]{:S(2)}) collective-permute-start(bf16[104,768]{1,0:T(8,128)(2,1)S(1)} %collective-permute-done.4.packed_ref), channel_id=1, source_target_pairs={{0,1},{1,0},{2,3},{3,2},{4,5},{5,4},{6,7},{7,6},{8,9},{9,8},{10,11... | collective-permute-start | bytes 479240 | tf_op jit(solution)/shard_map/ppermute | solution.py:237
  15.8 4.8 %collective-permute-start.6 = (f32[1,768]{1,0:T(1,128)S(1)}, f32[1,768]{1,0:T(1,128)S(1)}, u32[]{:S(2)}, u32[]{:S(2)}) collective-permute-start(f32[1,768]{1,0:T(1,128)S(1)} %score_far.1), channel_id=1, source_target_pairs={{0,8},{1,9},{2,10},{3,11},{4,12},{5,13},{6,14},{7,15},{8,0},{9,1},... | collective-permute-start | bytes 9224 | tf_op jit(solution)/shard_map/ppermute | solution.py:237
  20.6 1.5 %collective-permute-start.7 = (f32[1,384]{1,0:T(1,128)S(1)}, f32[1,384]{1,0:T(1,128)S(1)}, u32[]{:S(2)}, u32[]{:S(2)}) collective-permute-start(f32[1,384]{1,0:T(1,128)S(1)} %broadcast_select_fusion), channel_id=1, source_target_pairs={{0,1},{1,0},{2,3},{3,2},{4,5},{5,4},{6,7},{7,6},{8,9},{9,8},{10,11... | collective-permute-start | bytes 4616 | tf_op jit(solution)/shard_map/ppermute | solution.py:237

commit v4 on v3

v4 whole, which is shorter than its diff:
```python
import functools

import jax
import jax.numpy as jnp
from jax import lax
from jax.experimental import pallas as pl
from jax.experimental.pallas import tpu as pltpu
from jax.sharding import PartitionSpec as P

LANES = 128
META_ROWS = 8
VMEM_LIMIT = 8 * 1024 * 1024
BLOCK_SUBS = 16
STEP_LANES = 256
AXES = ("group", "tile")
GATHER = lax.GatherDimensionNumbers(
    offset_dims=(),
    collapsed_slice_dims=(1,),
    start_index_map=(1,),
    operand_batching_dims=(0,),
    start_indices_batching_dims=(0,),
)


def gather_lanes(table, index):
    return lax.gather(
        table, index[..., None], GATHER, slice_sizes=(1, 1), mode=lax.GatherScatterMode.PROMISE_IN_BOUNDS
    )


def integers(values):
    return values.astype(jnp.float32).astype(jnp.int32)


def read_keys(meta):
    meta = integers(meta)
    key = ((meta[3:4] * 256 + meta[2:3]) * 256 + meta[1:2]) * 256 + meta[0:1]
    return key, key - (meta[5:6] * 256 + meta[4:5])


def spread_keys(key, out_ref):
    for c in range(key.shape[1] // LANES):
        lanes = slice(c * LANES, (c + 1) * LANES)
        out_ref[lanes, :] = jnp.broadcast_to(key[:, lanes], (LANES, LANES)).T


def make_table(codebook_ref, table_ref, wide_ref, sub_dim):
    features = table_ref.shape[0]
    wide = codebook_ref[...].astype(jnp.float32).T
    for half in range(wide.shape[1] // LANES):
        lanes = slice(half * LANES, (half + 1) * LANES)
        wide_ref[...] = wide[:, lanes]
        for first in range(0, features, BLOCK_SUBS * sub_dim):
            for e in range(sub_dim):
                row = first + e * BLOCK_SUBS
                strided = wide_ref[pl.ds(first + e, BLOCK_SUBS, stride=sub_dim), :]
                table_ref[row : row + BLOCK_SUBS, lanes] = strided.astype(jnp.bfloat16)


def decode(codes, table_ref, exact_ref, out_ref, chunks=None):
    features = table_ref.shape[0]
    subs, rows = codes.shape
    sub_dim = features // subs
    for c in range(rows // LANES) if chunks is None else chunks:
        lanes = slice(c * LANES, (c + 1) * LANES)
        total = jnp.zeros((8, LANES), jnp.float32)
        for block in range(subs // BLOCK_SUBS):
            chosen = integers(codes[block * BLOCK_SUBS : (block + 1) * BLOCK_SUBS, lanes]).astype(jnp.int16)
            index = chosen & (LANES - 1)
            in_low = chosen < LANES
            for e in range(sub_dim):
                row = (block * sub_dim + e) * BLOCK_SUBS
                table = table_ref[row : row + BLOCK_SUBS, :]
                low, high = gather_lanes(table[:, :LANES], index), gather_lanes(table[:, LANES:], index)
                exact = jnp.where(in_low, low, high)
                exact_ref[row : row + BLOCK_SUBS, lanes] = exact
                square = exact.astype(jnp.float32)
                square = square * square
                total = total + square[:8] + square[8:]
        inverse = lax.rsqrt(jnp.sum(total, axis=0, keepdims=True) + 1e-06)
        inverse = jnp.broadcast_to(inverse, (BLOCK_SUBS, LANES))
        for row in range(0, features, BLOCK_SUBS):
            exact = exact_ref[row : row + BLOCK_SUBS, lanes].astype(jnp.float32)
            out_ref[row : row + BLOCK_SUBS, lanes] = (exact * inverse).astype(jnp.bfloat16)


def meta_rows(cluster, slot, group_slots, groups):
    local = slot
    for g in range(1, groups):
        local = local - jnp.where(slot >= g * group_slots, group_slots, 0)
    key = cluster * group_slots + local
    digits = [key & 255, (key >> 8) & 255, (key >> 16) & 255, key >> 24, local & 255, local >> 8]
    row = lax.broadcasted_iota(jnp.int32, (META_ROWS, key.shape[1]), 0)
    meta = jnp.zeros(row.shape, jnp.int32)
    for d, digit in enumerate(digits):
        meta = jnp.where(row == d, digit, meta)
    return meta.astype(jnp.float32).astype(jnp.bfloat16)


def pack(codes, cluster, slot, group_slots, groups):
    subs, rows = codes.shape
    meta = meta_rows(cluster.reshape(1, rows), slot.reshape(1, rows), group_slots, groups)
    return codes.astype(jnp.float32).astype(jnp.bfloat16), meta


def pack_kernel(group_slots, groups, *refs):
    sources, out_ref, buffers, sems = refs[:3], refs[3], refs[4:7], refs[7]
    copies = [
        pltpu.make_async_copy(source, buffer, sems.at[k]) for k, (source, buffer) in enumerate(zip(sources, buffers))
    ]
    for copy in copies:
        copy.start()
    for copy in copies:
        copy.wait()
    codes, meta = pack(*(buffer[...] for buffer in buffers), group_slots, groups)
    out_ref[: codes.shape[0], :] = codes
    out_ref[codes.shape[0] :, :] = meta


def join_kernel(group_slots, groups, packed_ref, codes_ref, cluster_ref, slot_ref, out_ref):
    subs, rows = codes_ref.shape
    codes, meta = pack(codes_ref[...], cluster_ref[...], slot_ref[...], group_slots, groups)
    out_ref[:, :rows] = packed_ref[...]
    out_ref[:subs, rows:] = codes
    out_ref[subs:, rows:] = meta


def unit_kernel(packed_ref, table_ref, out_ref, exact_ref):
    features = table_ref.shape[0]
    subs = packed_ref.shape[0] - META_ROWS
    decode(packed_ref[:subs, :], table_ref, exact_ref, out_ref)
    out_ref[features:, :] = packed_ref[subs:, :]


def turn(unit_ref, rows_ref, key_ref, base_ref):
    rows, features = rows_ref.shape
    rows_ref[...] = unit_ref[:features, :rows].T
    key, base = read_keys(unit_ref[features:, :rows])
    spread_keys(key, key_ref)
    spread_keys(base, base_ref)


def score(rows_ref, key_ref, base_ref, unit_refs, best):
    features = rows_ref.shape[1]
    for unit_ref in unit_refs:
        count = unit_ref.shape[1]
        column_key, _ = read_keys(unit_ref[features:, :])
        for first in range(0, count, STEP_LANES):
            span = slice(first, min(first + STEP_LANES, count))
            scores = jnp.dot(rows_ref[...], unit_ref[:features, span], preferred_element_type=jnp.float32)
            for c in range(0, scores.shape[1], LANES):
                keys = column_key[:, first + c : first + c + LANES]
                allowed = (keys < key_ref[...]) & (keys >= base_ref[...])
                best = jnp.maximum(best, jnp.where(allowed, scores[:, c : c + LANES], -1.0))
    return best


def nothing(shape):
    return jnp.full(shape, -1.0, jnp.float32)


def finish(best):
    rows = best.shape[0]
    pieces = [
        jnp.max(best[first : first + LANES, :].T, axis=0, keepdims=True) for first in range(0, rows, LANES)
    ]
    return jnp.concatenate(pieces, axis=1)


def own_kernel(codebook_ref, packed_ref, table_ref, unit_ref, rows_ref, key_ref, base_ref, wide_ref, exact_ref):
    subs = packed_ref.shape[0] - META_ROWS
    make_table(codebook_ref, table_ref, wide_ref, table_ref.shape[0] // subs)
    unit_kernel(packed_ref, table_ref, unit_ref, exact_ref)
    turn(unit_ref, rows_ref, key_ref, base_ref)


def far_kernel(packed_ref, table_ref, rows_ref, key_ref, base_ref, unit_ref, exact_ref):
    unit_kernel(packed_ref, table_ref, unit_ref, exact_ref)
    turn(unit_ref, rows_ref, key_ref, base_ref)


def step_kernel(plan, whole, *refs):
    refs = list(refs)
    take = lambda count: [refs.pop(0) for _ in range(count)]
    jobs = [(take(3), take(ready), take(1) if so_far else None) for ready, so_far in plan]
    if len(refs) > len(plan):
        table_ref, packed_ref, out_ref = take(3)
        unit_kernel(packed_ref, table_ref, out_ref, refs[-1])
    for (rows, unit_refs, so_far), best_ref in zip(jobs, refs):
        best = so_far[0][...] if so_far else nothing((rows[0].shape[0], LANES))
        best = score(*rows, unit_refs, best)
        best_ref[...] = finish(best) if whole else best


VMEM = pl.BlockSpec(memory_space=pltpu.MemorySpace.VMEM)
HBM = pl.BlockSpec(memory_space=pltpu.MemorySpace.HBM)


def call(kernel, microseconds, name, out_shape, scratch=(), in_spec=VMEM):
    def run(*operands):
        return pl.pallas_call(
            kernel,
            in_specs=[in_spec] * len(operands),
            out_shape=out_shape,
            scratch_shapes=scratch,
            compiler_params=pltpu.CompilerParams(vmem_limit_bytes=VMEM_LIMIT),
            cost_estimate=pl.CostEstimate(flops=int(microseconds * 1.15e9), bytes_accessed=0, transcendentals=0),
            name=name,
        )(*operands)

    return run


def body(product_codes, member_cluster, member_slot, codebook):
    row_count, subs = product_codes.shape
    code_count, features = codebook.shape
    groups = lax.axis_size("group")
    tiles = lax.axis_size("tile")
    devices = groups * tiles
    pair_rows = 2 * row_count
    group_slots = tiles * 2 * row_count
    packed_rows = subs + META_ROWS

    def exchange(value, offset_core0, offset_core1):
        pairs = [(i, i ^ (offset_core0 if i % 2 == 0 else offset_core1)) for i in range(devices)]
        return lax.ppermute(value, AXES, pairs)

    far = (groups // 2) * tiles
    chips = [dz * tiles + dx * 2 for dz in range(groups // 2) for dx in range(tiles // 2)]
    pairs, last_chip = list(zip(chips[1:-1:2], chips[2:-1:2])), chips[-1]

    shape = jax.ShapeDtypeStruct
    bf16 = jnp.bfloat16

    def exact(count):
        return pltpu.VMEM((features, count), bf16)

    def unit(count):
        return shape((features + META_ROWS, count), bf16)

    spread = shape((row_count, LANES), jnp.int32)
    turned = (shape((row_count, features), bf16), spread, spread)
    lane_best = shape((row_count, LANES), jnp.float32)
    row_best = shape((1, row_count), jnp.float32)

    mine = (product_codes, member_cluster, member_slot)
    other_codes, other_cluster, other_slot = (exchange(value, 1, 1) for value in mine)
    packed = call(
        functools.partial(pack_kernel, group_slots, groups),
        0.3,
        "pack",
        shape((packed_rows, row_count), bf16),
        [pltpu.VMEM((subs, row_count), jnp.int32)]
        + [pltpu.VMEM((row_count,), jnp.int32)] * 2
        + [pltpu.SemaphoreType.DMA((3,))],
        in_spec=HBM,
    )(*(pltpu.with_memory_space_constraint(v, pltpu.MemorySpace.HBM) for v in (product_codes.T, *mine[1:])))
    own = call(
        functools.partial(join_kernel, group_slots, groups), 0.3, "join", shape((packed_rows, pair_rows), bf16)
    )(packed, other_codes.T, other_cluster, other_slot)
    packed, own = lax.optimization_barrier((packed, own))
    from_far = exchange(packed, far, far)
    arrived = [exchange(own, *pair) for pair in pairs]
    last = exchange(packed, last_chip, last_chip)

    table, own_unit, *own_rows = call(
        own_kernel,
        1.4,
        "decode_own",
        (shape((features, code_count), bf16), unit(pair_rows), *turned),
        [pltpu.VMEM((features, LANES), jnp.float32), exact(pair_rows)],
    )(codebook, own)

    def step(name, jobs, packed=None, whole=False):
        out_shape = [row_best if whole else lane_best for _ in jobs]
        operands, plan, decode_time, score_time = [], [], 0.0, 0.0
        for rows, ready, so_far in jobs:
            operands += [*rows, *ready, *([] if so_far is None else [so_far])]
            plan.append((len(ready), so_far is not None))
            score_time += sum(u.shape[1] for u in ready) * 0.0007
        scratch = []
        if packed is not None:
            out_shape.insert(0, unit(packed.shape[1]))
            operands += [table, packed]
            decode_time = packed.shape[1] * 0.0011
            scratch = [exact(packed.shape[1])]
        kernel = functools.partial(step_kernel, plan, whole)
        return call(kernel, 0.2 + max(decode_time, score_time), name, out_shape, scratch)(*operands)

    first, table, own_unit = lax.optimization_barrier((arrived[0], table, own_unit))
    passed = exchange(first, 1, 1)
    first_unit, near_best = step("first", [(own_rows, [own_unit], None)], first)
    from_far, near_best = lax.optimization_barrier((from_far, near_best))
    far_rows = call(
        far_kernel, 0.9, "far", turned, [pltpu.VMEM(unit(row_count).shape, bf16), exact(row_count)]
    )(from_far, table)
    last, far_rows = lax.optimization_barrier((last, far_rows))
    last_passed = exchange(last, 1, 1)
    waiting, far_best = step("second", [(far_rows, [own_unit, first_unit], None)], passed)
    units = [first_unit, waiting]
    for latest in [codes for received in arrived[1:] for codes in (received, exchange(received, 1, 1))] + [last, last_passed]:
        waiting, far_best = step("more", [(far_rows, [waiting], far_best)], latest)
        units.append(waiting)
    (far_best,) = step("far_rest", [(far_rows, [waiting], far_best)], whole=True)
    best = exchange(far_best, far, far)
    for k in range(0, len(units), 4):
        (part,) = step("near_rest", [(own_rows, units[k : k + 4], near_best)], whole=True)
        best = jnp.maximum(best, part)
    return best.reshape(row_count)


def solution(mesh):
    placed = (
        P(("parts", "group", "tile"), None),
        P(("parts", "group", "tile")),
        P(("parts", "group", "tile")),
        P(),
    )
    return jax.shard_map(
        body, mesh=mesh, in_specs=placed, out_specs=P(("parts", "group", "tile")), check_vma=False
    )
```

time: 23.1 us -> 22.1 us (0.957); the launches traced: 22.7 us -> 22 us
  waiting for transfers between devices: 2.73 us -> 1.3 us
  Pallas kernels: 9.32 us -> 10 us
    ppermute x8 -> x9, waiting for transfers between devices: 2.73 us -> 1.3 us  [exchange(): return lax.ppermute(value, AXES, pairs)]
    pallas_call x7 -> x10, Pallas kernels: 9.32 us -> 10 us  [run(): pl.pallas_call(kernel, in_specs=[in_spec] * len(operands), out_shape=out_...]
    ppermute x8 -> x9, starting transfers between devices: 9.94 us -> 9.96 us  [exchange(): return lax.ppermute(value, AXES, pairs)]
    max x2 -> x1, other arithmetic: 0.6 us -> 0.6 us  [body(): best = jnp.maximum(best, part)]
  transfers between devices with their start and end apart: 8 -> 9, of which waited for: 3 -> 2; matrix products, arithmetic and copies ran while one was open for 0% -> 0% of each run, Pallas kernels for 31% -> 40%
where the time goes in v4:
time: 22.1 us; the launch traced here: 22 us
  Pallas kernels  10 us (45%)
  starting transfers between devices  9.96 us (45%)
  waiting for transfers between devices  1.3 us (6%)
  other arithmetic  0.6 us (3%)
    pallas_call x10, Pallas kernels, run(): pl.pallas_call(kernel, in_specs=[in_spec] * len(operands), out_shape=out_...  10 us
    ppermute x9, starting transfers between devices, exchange(): return lax.ppermute(value, AXES, pairs)  9.96 us
    ppermute x9, waiting for transfers between devices, exchange(): return lax.ppermute(value, AXES, pairs)  1.3 us
    max x1, other arithmetic, body(): best = jnp.maximum(best, part)  0.6 us
  transfers between devices with their start and end apart: 9, of which 2 were waited for; matrix products, arithmetic and copies ran while one was open for 0% of the time, Pallas kernels for 40%

profile of v4, /device:TPU:0, one launch (start us, length us, event | category | flops | bytes accessed | tf_op | source)
XLA Modules:
  0.0 22.0 jit_solution(10316346408176785177)
XLA Ops:
  0.0 0.5 %collective-permute-start = (s32[384,96]{0,1:T(8,128)}, s32[384,96]{0,1:T(8,128)S(1)}, u32[]{:S(2)}, u32[]{:S(2)}) collective-permute-start(s32[384,96]{0,1:T(8,128)} %param.4), channel_id=1, source_target_pairs={{0,1},{1,0},{2,3},{3,2},{4,5},{5,4},{6,7},{7,6},{8,9},{9,8},{10,11... | collective-permute-start | bytes 442376 | tf_op jit(solution)/shard_map/ppermute | solution.py:226
  0.5 0.1 collective-permute-start.1
  0.5 0.5 %collective-permute-start.2 = (s32[384]{0:T(512)}, s32[384]{0:T(512)S(1)}, u32[]{:S(2)}, u32[]{:S(2)}) collective-permute-start(s32[384]{0:T(512)} %refs_2_.1), channel_id=1, source_target_pairs={{0,1},{1,0},{2,3},{3,2},{4,5},{5,4},{6,7},{7,6},{8,9},{9,8},{10,11... | collective-permute-start | bytes 4616 | tf_op jit(solution)/shard_map/ppermute | solution.py:226
  1.0 0.0 copy-start
  1.0 1.0 %pack.1.packed_ref = bf16[104,384]{1,0:T(8,128)(2,1)S(1)} custom-call(s32[96,384]{1,0:T(8,128)} %bitcast.3, s32[384]{0:T(512)} %refs_1_.1, s32[384]{0:T(512)} %refs_2_.1), custom_call_target="tpu_custom_call" | custom-call | flops 345000000 | tf_op jit(solution)/shard_map/pack/pallas_call | solution.py:201
  2.0 0.0 collective-permute-done.1.cluster_ref
  2.0 0.0 collective-permute-done.2.slot_ref
  2.0 0.0 collective-permute-done
  2.1 2.9 %collective-permute-start.5 = (bf16[104,768]{1,0:T(8,128)(2,1)S(1)}, bf16[104,768]{1,0:T(8,128)(2,1)S(1)}, u32[]{:S(2)}, u32[]{:S(2)}) collective-permute-start(bf16[104,768]{1,0:T(8,128)(2,1)S(1)} %join.1.packed_ref), channel_id=1, source_target_pairs={{0,2},{1,5},{2,0},{3,7},{4,6},{5,1},{6,4},{7,3},{8,10},{9,13},{10,... | collective-permute-start | bytes 479240 | tf_op jit(solution)/shard_map/ppermute | solution.py:226
  4.9 2.6 %collective-permute-start.4 = (bf16[104,384]{1,0:T(8,128)(2,1)S(1)}, bf16[104,384]{1,0:T(8,128)(2,1)S(1)}, u32[]{:S(2)}, u32[]{:S(2)}) collective-permute-start(bf16[104,384]{1,0:T(8,128)(2,1)S(1)} %pack.1.packed_ref), channel_id=1, source_target_pairs={{0,8},{1,9},{2,10},{3,11},{4,12},{5,13},{6,14},{7,15},{8,0},{9,1},... | collective-permute-start | bytes 239624 | tf_op jit(solution)/shard_map/ppermute | solution.py:226
  7.5 1.5 %collective-permute-start.3 = (bf16[104,384]{1,0:T(8,128)(2,1)S(1)}, bf16[104,384]{1,0:T(8,128)(2,1)S(1)}, u32[]{:S(2)}, u32[]{:S(2)}) collective-permute-start(bf16[104,384]{1,0:T(8,128)(2,1)S(1)} %pack.1.packed_ref), channel_id=1, source_target_pairs={{0,6},{1,7},{2,4},{3,5},{4,2},{5,3},{6,0},{7,1},{8,14},{9,15},{10,... | collective-permute-start | bytes 239624 | tf_op jit(solution)/shard_map/ppermute | solution.py:226
  9.1 0.0 copy-done
  9.1 1.4 %decode_own.1 = (bf16[768,256]{1,0:T(8,128)(2,1)S(1)}, bf16[776,768]{1,0:T(8,128)(2,1)S(1)}, bf16[384,768]{1,0:T(8,128)(2,1)S(1)}, s32[384,128]{1,0:T(8,128)S(1)}, s32[384,128]{1,0:T(8,128)S(1)}) custom-call(bf16[256,768]{1,0:T(8,128)(2,1)S(1)} %copy-done, bf16[104,768]{1,0:T(8,128)(2,1)S(1)} %join.1.packed_ref), custom_call_target="tpu_custom_call" | custom-call | flops 1610000000 | tf_op jit(solution)/shard_map/decode_own/pallas_call | solution.py:201
  10.4 0.0 collective-permute-done.5.refs_5_
  10.5 0.1 collective-permute-start.6
  10.5 1.2 %first.1 = (bf16[776,768]{1,0:T(8,128)(2,1)S(1)}, f32[384,128]{1,0:T(8,128)S(1)}) custom-call(bf16[384,768]{1,0:T(8,128)(2,1)S(1)} %get-tuple-element.34.refs_0_, s32[384,128]{1,0:T(8,128)S(1)} %get-tuple-element.35.refs_1_, s32[384,128]{1,0:T(8,128)S(1)} %get-tuple-element.36.refs_2_, bf16[776,768]{1,0:T(8,128)(2,1)S(1)} %get-tuple-element.39.refs_3_, ...), custom_call_target="tpu_custom_call" | custom-call | flops 1201520000 | tf_op jit(solution)/shard_map/first/pallas_call | solution.py:201
  11.8 0.0 collective-permute-done.4.packed_ref
  11.8 0.8 %far.1 = (bf16[384,768]{1,0:T(8,128)(2,1)S(1)}, s32[384,128]{1,0:T(8,128)S(1)}, s32[384,128]{1,0:T(8,128)S(1)}) custom-call(bf16[104,384]{1,0:T(8,128)(2,1)S(1)} %collective-permute-done.4.packed_ref, bf16[768,256]{1,0:T(8,128)(2,1)S(1)} %get-tuple-element.40.refs_4_.table_ref.refs_5_), custom_call_target="tpu_custom_call" | custom-call | flops 1035000000 | tf_op jit(solution)/shard_map/far/pallas_call | solution.py:201
  12.6 0.2 %collective-permute-done.3.refs_6_ = bf16[104,384]{1,0:T(8,128)(2,1)S(1)} collective-permute-done((bf16[104,384]{1,0:T(8,128)(2,1)S(1)}, bf16[104,384]{1,0:T(8,128)(2,1)S(1)}, u32[]{:S(2)}, u32[]{:S(2)}) %collective-permute-start.3) | collective-permute-done | bytes 79904 | tf_op jit(solution)/shard_map/ppermute | solution.py:226
  12.8 0.3 %collective-permute-start.7 = (bf16[104,384]{1,0:T(8,128)(2,1)S(1)}, bf16[104,384]{1,0:T(8,128)(2,1)S(1)}, u32[]{:S(2)}, u32[]{:S(2)}) collective-permute-start(bf16[104,384]{1,0:T(8,128)(2,1)S(1)} %collective-permute-done.3.refs_6_), channel_id=1, source_target_pairs={{0,1},{1,0},{2,3},{3,2},{4,5},{5,4},{6,7},{7,6},{8,9},{9,8},{10,11... | collective-permute-start | bytes 239624 | tf_op jit(solution)/shard_map/ppermute | solution.py:226
  13.2 0.0 collective-permute-done.6.refs_6_
  13.2 1.6 %second.1 = (bf16[776,768]{1,0:T(8,128)(2,1)S(1)}, f32[384,128]{1,0:T(8,128)S(1)}) custom-call(bf16[384,768]{1,0:T(8,128)(2,1)S(1)} %get-tuple-element.47.refs_0_, s32[384,128]{1,0:T(8,128)S(1)} %get-tuple-element.48.refs_1_, s32[384,128]{1,0:T(8,128)S(1)} %get-tuple-element.49.refs_2_, bf16[776,768]{1,0:T(8,128)(2,1)S(1)} %get-tuple-element.39.refs_3_, ...), custom_call_target="tpu_custom_call" | custom-call | flops 1466480000 | tf_op jit(solution)/shard_map/second/pallas_call | solution.py:201
  14.7 0.9 %more.2 = (bf16[776,384]{1,0:T(8,128)(2,1)S(1)}, f32[384,128]{1,0:T(8,128)S(1)}) custom-call(bf16[384,768]{1,0:T(8,128)(2,1)S(1)} %get-tuple-element.47.refs_0_, s32[384,128]{1,0:T(8,128)S(1)} %get-tuple-element.48.refs_1_, s32[384,128]{1,0:T(8,128)S(1)} %get-tuple-element.49.refs_2_, bf16[776,768]{1,0:T(8,128)(2,1)S(1)} %get-tuple-element.51.refs_3_.refs_4_, ...), custom_call_target="tpu_custom_call" | custom-call | flops 848240000 | tf_op jit(solution)/shard_map/more/pallas_call | solution.py:201
  15.6 0.0 collective-permute-done.7.refs_6_
  15.6 0.7 %more.3 = (bf16[776,384]{1,0:T(8,128)(2,1)S(1)}, f32[384,128]{1,0:T(8,128)S(1)}) custom-call(bf16[384,768]{1,0:T(8,128)(2,1)S(1)} %get-tuple-element.47.refs_0_, s32[384,128]{1,0:T(8,128)S(1)} %get-tuple-element.48.refs_1_, s32[384,128]{1,0:T(8,128)S(1)} %get-tuple-element.49.refs_2_, bf16[776,384]{1,0:T(8,128)(2,1)S(1)} %get-tuple-element.54.refs_3_.refs_5_, ...), custom_call_target="tpu_custom_call" | custom-call | flops 715760000 | tf_op jit(solution)/shard_map/more/pallas_call | solution.py:201
  16.3 0.6 %far_rest.1 = f32[1,384]{1,0:T(1,128)S(1)} custom-call(bf16[384,768]{1,0:T(8,128)(2,1)S(1)} %get-tuple-element.47.refs_0_, s32[384,128]{1,0:T(8,128)S(1)} %get-tuple-element.48.refs_1_, s32[384,128]{1,0:T(8,128)S(1)} %get-tuple-element.49.refs_2_, bf16[776,384]{1,0:T(8,128)(2,1)S(1)} %get-tuple-element.56.refs_3_.refs_6_, ...), custom_call_target="tpu_custom_call" | custom-call | flops 539120000 | tf_op jit(solution)/shard_map/far_rest/pallas_call | solution.py:201
  16.8 1.6 %collective-permute-start.8 = (f32[1,384]{1,0:T(1,128)S(1)}, f32[1,384]{1,0:T(1,128)S(1)}, u32[]{:S(2)}, u32[]{:S(2)}) collective-permute-start(f32[1,384]{1,0:T(1,128)S(1)} %far_rest.1), channel_id=1, source_target_pairs={{0,8},{1,9},{2,10},{3,11},{4,12},{5,13},{6,14},{7,15},{8,0},{9,1},... | collective-permute-start | bytes 4616 | tf_op jit(solution)/shard_map/ppermute | solution.py:226
  18.4 1.9 %near_rest.1 = f32[1,384]{1,0:T(1,128)S(1)} custom-call(bf16[384,768]{1,0:T(8,128)(2,1)S(1)} %get-tuple-element.34.refs_0_, s32[384,128]{1,0:T(8,128)S(1)} %get-tuple-element.35.refs_1_, s32[384,128]{1,0:T(8,128)S(1)} %get-tuple-element.36.refs_2_, bf16[776,768]{1,0:T(8,128)(2,1)S(1)} %get-tuple-element.50.refs_4_.refs_3_, ...), custom_call_target="tpu_custom_call" | custom-call | flops 2084720000 | tf_op jit(solution)/shard_map/near_rest/pallas_call | solution.py:201
  20.3 1.0 %collective-permute-done.8 = f32[1,384]{1,0:T(1,128)S(1)} collective-permute-done((f32[1,384]{1,0:T(1,128)S(1)}, f32[1,384]{1,0:T(1,128)S(1)}, u32[]{:S(2)}, u32[]{:S(2)}) %collective-permute-start.8) | collective-permute-done | bytes 1568 | tf_op jit(solution)/shard_map/ppermute | solution.py:226
  21.4 0.6 %maximum_reduce_fusion = f32[384]{0:T(512)} fusion(f32[1,384]{1,0:T(1,128)S(1)} %collective-permute-done.8, f32[1,384]{1,0:T(1,128)S(1)} %near_rest.1), kind=kLoop, calls=%fused_computation | loop fusion | flops 384 | bytes 4608 | tf_op jit(solution)/shard_map/max | solution.py:308
  (1 shorter events, 0.0 us)
Async XLA Ops:
  0.0 2.0 %collective-permute-start = (s32[384,96]{0,1:T(8,128)}, s32[384,96]{0,1:T(8,128)S(1)}, u32[]{:S(2)}, u32[]{:S(2)}) collective-permute-start(s32[384,96]{0,1:T(8,128)} %param.4), channel_id=1, source_target_pairs={{0,1},{1,0},{2,3},{3,2},{4,5},{5,4},{6,7},{7,6},{8,9},{9,8},{10,11... | collective-permute-start | bytes 442376 | tf_op jit(solution)/shard_map/ppermute | solution.py:226
  0.5 1.5 %collective-permute-start.1 = (s32[384]{0:T(512)}, s32[384]{0:T(512)S(1)}, u32[]{:S(2)}, u32[]{:S(2)}) collective-permute-start(s32[384]{0:T(512)} %refs_1_.1), channel_id=1, source_target_pairs={{0,1},{1,0},{2,3},{3,2},{4,5},{5,4},{6,7},{7,6},{8,9},{9,8},{10,11... | collective-permute-start | bytes 4616 | tf_op jit(solution)/shard_map/ppermute | solution.py:226
  0.5 1.5 %collective-permute-start.2 = (s32[384]{0:T(512)}, s32[384]{0:T(512)S(1)}, u32[]{:S(2)}, u32[]{:S(2)}) collective-permute-start(s32[384]{0:T(512)} %refs_2_.1), channel_id=1, source_target_pairs={{0,1},{1,0},{2,3},{3,2},{4,5},{5,4},{6,7},{7,6},{8,9},{9,8},{10,11... | collective-permute-start | bytes 4616 | tf_op jit(solution)/shard_map/ppermute | solution.py:226
  1.0 8.1 %copy-start = (bf16[256,768]{1,0:T(8,128)(2,1)S(1)}, bf16[256,768]{1,0:T(8,128)(2,1)}, u32[]{:S(2)}) copy-start(bf16[256,768]{1,0:T(8,128)(2,1)} %codebook_ref.1) | copy-start | bytes 1179652
  2.1 8.4 %collective-permute-start.5 = (bf16[104,768]{1,0:T(8,128)(2,1)S(1)}, bf16[104,768]{1,0:T(8,128)(2,1)S(1)}, u32[]{:S(2)}, u32[]{:S(2)}) collective-permute-start(bf16[104,768]{1,0:T(8,128)(2,1)S(1)} %join.1.packed_ref), channel_id=1, source_target_pairs={{0,2},{1,5},{2,0},{3,7},{4,6},{5,1},{6,4},{7,3},{8,10},{9,13},{10,... | collective-permute-start | bytes 479240 | tf_op jit(solution)/shard_map/ppermute | solution.py:226
  4.9 6.8 %collective-permute-start.4 = (bf16[104,384]{1,0:T(8,128)(2,1)S(1)}, bf16[104,384]{1,0:T(8,128)(2,1)S(1)}, u32[]{:S(2)}, u32[]{:S(2)}) collective-permute-start(bf16[104,384]{1,0:T(8,128)(2,1)S(1)} %pack.1.packed_ref), channel_id=1, source_target_pairs={{0,8},{1,9},{2,10},{3,11},{4,12},{5,13},{6,14},{7,15},{8,0},{9,1},... | collective-permute-start | bytes 239624 | tf_op jit(solution)/shard_map/ppermute | solution.py:226
  7.5 5.3 %collective-permute-start.3 = (bf16[104,384]{1,0:T(8,128)(2,1)S(1)}, bf16[104,384]{1,0:T(8,128)(2,1)S(1)}, u32[]{:S(2)}, u32[]{:S(2)}) collective-permute-start(bf16[104,384]{1,0:T(8,128)(2,1)S(1)} %pack.1.packed_ref), channel_id=1, source_target_pairs={{0,6},{1,7},{2,4},{3,5},{4,2},{5,3},{6,0},{7,1},{8,14},{9,15},{10,... | collective-permute-start | bytes 239624 | tf_op jit(solution)/shard_map/ppermute | solution.py:226
  10.5 2.7 %collective-permute-start.6 = (bf16[104,768]{1,0:T(8,128)(2,1)S(1)}, bf16[104,768]{1,0:T(8,128)(2,1)S(1)}, u32[]{:S(2)}, u32[]{:S(2)}) collective-permute-start(bf16[104,768]{1,0:T(8,128)(2,1)S(1)} %collective-permute-done.5.refs_5_), channel_id=1, source_target_pairs={{0,1},{1,0},{2,3},{3,2},{4,5},{5,4},{6,7},{7,6},{8,9},{9,8},{10,11... | collective-permute-start | bytes 479240 | tf_op jit(solution)/shard_map/ppermute | solution.py:226
  12.8 2.8 %collective-permute-start.7 = (bf16[104,384]{1,0:T(8,128)(2,1)S(1)}, bf16[104,384]{1,0:T(8,128)(2,1)S(1)}, u32[]{:S(2)}, u32[]{:S(2)}) collective-permute-start(bf16[104,384]{1,0:T(8,128)(2,1)S(1)} %collective-permute-done.3.refs_6_), channel_id=1, source_target_pairs={{0,1},{1,0},{2,3},{3,2},{4,5},{5,4},{6,7},{7,6},{8,9},{9,8},{10,11... | collective-permute-start | bytes 239624 | tf_op jit(solution)/shard_map/ppermute | solution.py:226
  16.8 4.5 %collective-permute-start.8 = (f32[1,384]{1,0:T(1,128)S(1)}, f32[1,384]{1,0:T(1,128)S(1)}, u32[]{:S(2)}, u32[]{:S(2)}) collective-permute-start(f32[1,384]{1,0:T(1,128)S(1)} %far_rest.1), channel_id=1, source_target_pairs={{0,8},{1,9},{2,10},{3,11},{4,12},{5,13},{6,14},{7,15},{8,0},{9,1},... | collective-permute-start | bytes 4616 | tf_op jit(solution)/shard_map/ppermute | solution.py:226

commit v5 on v4

--- a/solution.py
+++ b/solution.py
@@ -57,12 +57,13 @@
                 table_ref[row : row + BLOCK_SUBS, lanes] = strided.astype(jnp.bfloat16)
 
 
-def decode(codes, table_ref, exact_ref, out_ref, chunks=None):
+def decode(codes, table_ref, exact_ref, out_ref, column0):
     features = table_ref.shape[0]
     subs, rows = codes.shape
     sub_dim = features // subs
-    for c in range(rows // LANES) if chunks is None else chunks:
+    for c in range(rows // LANES):
         lanes = slice(c * LANES, (c + 1) * LANES)
+        out_lanes = slice(column0 + c * LANES, column0 + (c + 1) * LANES)
         total = jnp.zeros((8, LANES), jnp.float32)
         for block in range(subs // BLOCK_SUBS):
             chosen = integers(codes[block * BLOCK_SUBS : (block + 1) * BLOCK_SUBS, lanes]).astype(jnp.int16)
@@ -81,7 +82,7 @@
         inverse = jnp.broadcast_to(inverse, (BLOCK_SUBS, LANES))
         for row in range(0, features, BLOCK_SUBS):
             exact = exact_ref[row : row + BLOCK_SUBS, lanes].astype(jnp.float32)
-            out_ref[row : row + BLOCK_SUBS, lanes] = (exact * inverse).astype(jnp.bfloat16)
+            out_ref[row : row + BLOCK_SUBS, out_lanes] = (exact * inverse).astype(jnp.bfloat16)
 
 
 def meta_rows(cluster, slot, group_slots, groups):
@@ -125,22 +126,22 @@
     out_ref[subs:, rows:] = meta
 
 
-def unit_kernel(packed_ref, table_ref, out_ref, exact_ref):
+def unit_kernel(packed_ref, table_ref, out_ref, exact_ref, column0=0):
     features = table_ref.shape[0]
-    subs = packed_ref.shape[0] - META_ROWS
-    decode(packed_ref[:subs, :], table_ref, exact_ref, out_ref)
-    out_ref[features:, :] = packed_ref[subs:, :]
-
-
-def turn(unit_ref, rows_ref, key_ref, base_ref):
+    subs, rows = packed_ref.shape[0] - META_ROWS, packed_ref.shape[1]
+    decode(packed_ref[:subs, :], table_ref, exact_ref, out_ref, column0)
+    out_ref[features:, column0 : column0 + rows] = packed_ref[subs:, :]
+
+
+def turn(unit_ref, rows_ref, base_ref, slot_ref):
     rows, features = rows_ref.shape
     rows_ref[...] = unit_ref[:features, :rows].T
     key, base = read_keys(unit_ref[features:, :rows])
-    spread_keys(key, key_ref)
     spread_keys(base, base_ref)
-
-
-def score(rows_ref, key_ref, base_ref, unit_refs, best):
+    spread_keys(key - base, slot_ref)
+
+
+def score(rows_ref, base_ref, slot_ref, unit_refs, best):
     features = rows_ref.shape[1]
     for unit_ref in unit_refs:
         count = unit_ref.shape[1]
@@ -149,8 +150,8 @@
             span = slice(first, min(first + STEP_LANES, count))
             scores = jnp.dot(rows_ref[...], unit_ref[:features, span], preferred_element_type=jnp.float32)
             for c in range(0, scores.shape[1], LANES):
-                keys = column_key[:, first + c : first + c + LANES]
-                allowed = (keys < key_ref[...]) & (keys >= base_ref[...])
+                distance = column_key[:, first + c : first + c + LANES] - base_ref[...]
+                allowed = distance.astype(jnp.uint32) < slot_ref[...].astype(jnp.uint32)
                 best = jnp.maximum(best, jnp.where(allowed, scores[:, c : c + LANES], -1.0))
     return best
 
@@ -167,11 +168,21 @@
     return jnp.concatenate(pieces, axis=1)
 
 
-def own_kernel(codebook_ref, packed_ref, table_ref, unit_ref, rows_ref, key_ref, base_ref, wide_ref, exact_ref):
+def own_kernel(codebook_ref, packed_ref, table_ref, unit_ref, wide_ref, exact_ref):
     subs = packed_ref.shape[0] - META_ROWS
     make_table(codebook_ref, table_ref, wide_ref, table_ref.shape[0] // subs)
     unit_kernel(packed_ref, table_ref, unit_ref, exact_ref)
-    turn(unit_ref, rows_ref, key_ref, base_ref)
+
+
+def decode_kernel(*refs):
+    packed_ref, table_ref, unit_ref, exact_ref = refs
+    unit_kernel(packed_ref, table_ref, unit_ref, exact_ref)
+
+
+def near_kernel(own_ref, *refs):
+    *unit_refs, best_ref, rows_ref, key_ref, base_ref = refs
+    turn(own_ref, rows_ref, key_ref, base_ref)
+    best_ref[...] = finish(score(rows_ref, key_ref, base_ref, unit_refs, nothing(key_ref.shape)))
 
 
 def far_kernel(packed_ref, table_ref, rows_ref, key_ref, base_ref, unit_ref, exact_ref):
@@ -179,17 +190,18 @@
     turn(unit_ref, rows_ref, key_ref, base_ref)
 
 
-def step_kernel(plan, whole, *refs):
+def step_kernel(ready, with_so_far, decoded, whole, *refs):
     refs = list(refs)
     take = lambda count: [refs.pop(0) for _ in range(count)]
-    jobs = [(take(3), take(ready), take(1) if so_far else None) for ready, so_far in plan]
-    if len(refs) > len(plan):
-        table_ref, packed_ref, out_ref = take(3)
-        unit_kernel(packed_ref, table_ref, out_ref, refs[-1])
-    for (rows, unit_refs, so_far), best_ref in zip(jobs, refs):
-        best = so_far[0][...] if so_far else nothing((rows[0].shape[0], LANES))
-        best = score(*rows, unit_refs, best)
-        best_ref[...] = finish(best) if whole else best
+    rows, unit_refs, so_far = take(3), take(ready), take(with_so_far)
+    table_refs, packed_refs, out_refs = take(min(decoded, 1)), take(decoded), take(min(decoded, 1))
+    best_ref, exact_refs = refs[0], refs[1:]
+    column0 = 0
+    for packed_ref, exact_ref in zip(packed_refs, exact_refs):
+        unit_kernel(packed_ref, table_refs[0], out_refs[0], exact_ref, column0)
+        column0 += packed_ref.shape[1]
+    best = score(*rows, unit_refs, so_far[0][...] if so_far else nothing((rows[0].shape[0], LANES)))
+    best_ref[...] = finish(best) if whole else best
 
 
 VMEM = pl.BlockSpec(memory_space=pltpu.MemorySpace.VMEM)
@@ -263,48 +275,54 @@
     arrived = [exchange(own, *pair) for pair in pairs]
     last = exchange(packed, last_chip, last_chip)
 
-    table, own_unit, *own_rows = call(
+    table, own_unit = call(
         own_kernel,
         1.4,
         "decode_own",
-        (shape((features, code_count), bf16), unit(pair_rows), *turned),
+        (shape((features, code_count), bf16), unit(pair_rows)),
         [pltpu.VMEM((features, LANES), jnp.float32), exact(pair_rows)],
     )(codebook, own)
 
-    def step(name, jobs, packed=None, whole=False):
-        out_shape = [row_best if whole else lane_best for _ in jobs]
-        operands, plan, decode_time, score_time = [], [], 0.0, 0.0
-        for rows, ready, so_far in jobs:
-            operands += [*rows, *ready, *([] if so_far is None else [so_far])]
-            plan.append((len(ready), so_far is not None))
-            score_time += sum(u.shape[1] for u in ready) * 0.0007
-        scratch = []
-        if packed is not None:
-            out_shape.insert(0, unit(packed.shape[1]))
-            operands += [table, packed]
-            decode_time = packed.shape[1] * 0.0011
-            scratch = [exact(packed.shape[1])]
-        kernel = functools.partial(step_kernel, plan, whole)
-        return call(kernel, 0.2 + max(decode_time, score_time), name, out_shape, scratch)(*operands)
+    def decoded(name, packed):
+        count = packed.shape[1]
+        return call(decode_kernel, count * 0.0012, name, unit(count), [exact(count)])(packed, table)
+
+    def step(name, ready, packed, so_far=None, whole=False):
+        counts = [p.shape[1] for p in packed]
+        before = [] if so_far is None else [so_far]
+        operands = [*far_rows, *ready, *before, *([table] if packed else []), *packed]
+        time = 0.2 + max(sum(counts) * 0.0011, sum(u.shape[1] for u in ready) * 0.0007)
+        *more, best = call(
+            functools.partial(step_kernel, len(ready), len(before), len(packed), whole),
+            time,
+            name,
+            [*([unit(sum(counts))] if counts else []), row_best if whole else lane_best],
+            [exact(count) for count in counts],
+        )(*operands)
+        return more, best
 
     first, table, own_unit = lax.optimization_barrier((arrived[0], table, own_unit))
     passed = exchange(first, 1, 1)
-    first_unit, near_best = step("first", [(own_rows, [own_unit], None)], first)
-    from_far, near_best = lax.optimization_barrier((from_far, near_best))
+    first_unit = decoded("first", first)
+    from_far, first_unit = lax.optimization_barrier((from_far, first_unit))
     far_rows = call(
         far_kernel, 0.9, "far", turned, [pltpu.VMEM(unit(row_count).shape, bf16), exact(row_count)]
     )(from_far, table)
     last, far_rows = lax.optimization_barrier((last, far_rows))
     last_passed = exchange(last, 1, 1)
-    waiting, far_best = step("second", [(far_rows, [own_unit, first_unit], None)], passed)
-    units = [first_unit, waiting]
-    for latest in [codes for received in arrived[1:] for codes in (received, exchange(received, 1, 1))] + [last, last_passed]:
-        waiting, far_best = step("more", [(far_rows, [waiting], far_best)], latest)
-        units.append(waiting)
-    (far_best,) = step("far_rest", [(far_rows, [waiting], far_best)], whole=True)
+    (passed_unit,), far_best = step("second", [own_unit, first_unit], [passed])
+    (last_unit,), far_best = step("last", [passed_unit], [last, last_passed], far_best)
+    units = [own_unit, first_unit, passed_unit, last_unit]
+    rest = [last_unit]
+    for latest in [codes for received in arrived[1:] for codes in (received, exchange(received, 1, 1))]:
+        (more,), far_best = step("more", rest, [latest], far_best)
+        rest = [more]
+        units.append(more)
+    _, far_best = step("far_rest", rest, [], far_best, whole=True)
     best = exchange(far_best, far, far)
+    turned_scratch = [pltpu.VMEM(t.shape, t.dtype) for t in turned]
     for k in range(0, len(units), 4):
-        (part,) = step("near_rest", [(own_rows, units[k : k + 4], near_best)], whole=True)
+        part = call(near_kernel, 2.5, "near", row_best, turned_scratch)(own_unit, *units[k : k + 4])
         best = jnp.maximum(best, part)
     return best.reshape(row_count)
 

time: 22.1 us -> 21.5 us (0.973)
  Pallas kernels: 10 us -> 9.39 us
    pallas_call x10 -> x9, Pallas kernels: 10 us -> 9.39 us  [run(): pl.pallas_call(kernel, in_specs=[in_spec] * len(operands), out_shape=out_...]
  transfers between devices with their start and end apart: 9 -> 9, of which waited for: 2 -> 3; matrix products, arithmetic and copies ran while one was open for 0% -> 0% of each run, Pallas kernels for 40% -> 35%
where the time goes in v5:
time: 21.5 us; the launch traced here: 21.4 us
  starting transfers between devices  9.96 us (46%)
  Pallas kernels  9.39 us (44%)
  waiting for transfers between devices  1.31 us (6%)
  other arithmetic  0.6 us (3%)
    ppermute x9, starting transfers between devices, exchange(): return lax.ppermute(value, AXES, pairs)  9.96 us
    pallas_call x9, Pallas kernels, run(): pl.pallas_call(kernel, in_specs=[in_spec] * len(operands), out_shape=out_...  9.39 us
    ppermute x9, waiting for transfers between devices, exchange(): return lax.ppermute(value, AXES, pairs)  1.31 us
    max x1, other arithmetic, body(): best = jnp.maximum(best, part)  0.6 us
  transfers between devices with their start and end apart: 9, of which 3 were waited for; matrix products, arithmetic and copies ran while one was open for 0% of the time, Pallas kernels for 35%

profile of v5, /device:TPU:0, one launch (start us, length us, event | category | flops | bytes accessed | tf_op | source)
XLA Modules:
  0.0 21.4 jit_solution(16490542263138855031)
XLA Ops:
  0.0 0.5 %collective-permute-start = (s32[384,96]{0,1:T(8,128)}, s32[384,96]{0,1:T(8,128)S(1)}, u32[]{:S(2)}, u32[]{:S(2)}) collective-permute-start(s32[384,96]{0,1:T(8,128)} %param.4), channel_id=1, source_target_pairs={{0,1},{1,0},{2,3},{3,2},{4,5},{5,4},{6,7},{7,6},{8,9},{9,8},{10,11... | collective-permute-start | bytes 442376 | tf_op jit(solution)/shard_map/ppermute | solution.py:238
  0.5 0.1 collective-permute-start.1
  0.5 0.5 %collective-permute-start.2 = (s32[384]{0:T(512)}, s32[384]{0:T(512)S(1)}, u32[]{:S(2)}, u32[]{:S(2)}) collective-permute-start(s32[384]{0:T(512)} %refs_2_.1), channel_id=1, source_target_pairs={{0,1},{1,0},{2,3},{3,2},{4,5},{5,4},{6,7},{7,6},{8,9},{9,8},{10,11... | collective-permute-start | bytes 4616 | tf_op jit(solution)/shard_map/ppermute | solution.py:238
  1.0 0.0 copy-start
  1.0 1.0 %pack.1.packed_ref = bf16[104,384]{1,0:T(8,128)(2,1)S(1)} custom-call(s32[96,384]{1,0:T(8,128)} %bitcast.3, s32[384]{0:T(512)} %refs_1_.1, s32[384]{0:T(512)} %refs_2_.1), custom_call_target="tpu_custom_call" | custom-call | flops 345000000 | tf_op jit(solution)/shard_map/pack/pallas_call | solution.py:213
  2.0 0.0 collective-permute-done.1.cluster_ref
  2.0 0.0 collective-permute-done.2.slot_ref
  2.0 0.0 collective-permute-done
  2.1 2.9 %collective-permute-start.5 = (bf16[104,768]{1,0:T(8,128)(2,1)S(1)}, bf16[104,768]{1,0:T(8,128)(2,1)S(1)}, u32[]{:S(2)}, u32[]{:S(2)}) collective-permute-start(bf16[104,768]{1,0:T(8,128)(2,1)S(1)} %join.1.packed_ref), channel_id=1, source_target_pairs={{0,2},{1,5},{2,0},{3,7},{4,6},{5,1},{6,4},{7,3},{8,10},{9,13},{10,... | collective-permute-start | bytes 479240 | tf_op jit(solution)/shard_map/ppermute | solution.py:238
  4.9 2.6 %collective-permute-start.4 = (bf16[104,384]{1,0:T(8,128)(2,1)S(1)}, bf16[104,384]{1,0:T(8,128)(2,1)S(1)}, u32[]{:S(2)}, u32[]{:S(2)}) collective-permute-start(bf16[104,384]{1,0:T(8,128)(2,1)S(1)} %pack.1.packed_ref), channel_id=1, source_target_pairs={{0,8},{1,9},{2,10},{3,11},{4,12},{5,13},{6,14},{7,15},{8,0},{9,1},... | collective-permute-start | bytes 239624 | tf_op jit(solution)/shard_map/ppermute | solution.py:238
  7.5 1.5 %collective-permute-start.3 = (bf16[104,384]{1,0:T(8,128)(2,1)S(1)}, bf16[104,384]{1,0:T(8,128)(2,1)S(1)}, u32[]{:S(2)}, u32[]{:S(2)}) collective-permute-start(bf16[104,384]{1,0:T(8,128)(2,1)S(1)} %pack.1.packed_ref), channel_id=1, source_target_pairs={{0,6},{1,7},{2,4},{3,5},{4,2},{5,3},{6,0},{7,1},{8,14},{9,15},{10,... | collective-permute-start | bytes 239624 | tf_op jit(solution)/shard_map/ppermute | solution.py:238
  9.1 0.0 copy-done
  9.1 1.1 %decode_own.1 = (bf16[768,256]{1,0:T(8,128)(2,1)S(1)}, bf16[776,768]{1,0:T(8,128)(2,1)S(1)}) custom-call(bf16[256,768]{1,0:T(8,128)(2,1)S(1)} %copy-done, bf16[104,768]{1,0:T(8,128)(2,1)S(1)} %join.1.packed_ref), custom_call_target="tpu_custom_call" | custom-call | flops 1610000000 | tf_op jit(solution)/shard_map/decode_own/pallas_call | solution.py:213
  10.2 0.0 collective-permute-done.5.refs_0_
  10.2 0.1 collective-permute-start.6
  10.3 0.9 %first.1.refs_4_.refs_1_ = bf16[776,768]{1,0:T(8,128)(2,1)S(1)} custom-call(bf16[104,768]{1,0:T(8,128)(2,1)S(1)} %collective-permute-done.5.refs_0_, bf16[768,256]{1,0:T(8,128)(2,1)S(1)} %get-tuple-element.30.refs_1_.table_ref.refs_5_), custom_call_target="tpu_custom_call" | custom-call | flops 1059840000 | tf_op jit(solution)/shard_map/first/pallas_call | solution.py:213
  11.2 0.5 %collective-permute-done.4.packed_ref = bf16[104,384]{1,0:T(8,128)(2,1)S(1)} collective-permute-done((bf16[104,384]{1,0:T(8,128)(2,1)S(1)}, bf16[104,384]{1,0:T(8,128)(2,1)S(1)}, u32[]{:S(2)}, u32[]{:S(2)}) %collective-permute-start.4) | collective-permute-done | bytes 79904 | tf_op jit(solution)/shard_map/ppermute | solution.py:238
  11.7 0.8 %far.1 = (bf16[384,768]{1,0:T(8,128)(2,1)S(1)}, s32[384,128]{1,0:T(8,128)S(1)}, s32[384,128]{1,0:T(8,128)S(1)}) custom-call(bf16[104,384]{1,0:T(8,128)(2,1)S(1)} %collective-permute-done.4.packed_ref, bf16[768,256]{1,0:T(8,128)(2,1)S(1)} %get-tuple-element.30.refs_1_.table_ref.refs_5_), custom_call_target="tpu_custom_call" | custom-call | flops 1035000000 | tf_op jit(solution)/shard_map/far/pallas_call | solution.py:213
  12.5 0.3 %collective-permute-done.3.refs_6_ = bf16[104,384]{1,0:T(8,128)(2,1)S(1)} collective-permute-done((bf16[104,384]{1,0:T(8,128)(2,1)S(1)}, bf16[104,384]{1,0:T(8,128)(2,1)S(1)}, u32[]{:S(2)}, u32[]{:S(2)}) %collective-permute-start.3) | collective-permute-done | bytes 79904 | tf_op jit(solution)/shard_map/ppermute | solution.py:238
  12.8 0.0 collective-permute-start.7
  12.8 0.0 collective-permute-done.6.refs_6_
  12.8 1.5 %second.1 = (bf16[776,768]{1,0:T(8,128)(2,1)S(1)}, f32[384,128]{1,0:T(8,128)S(1)}) custom-call(bf16[384,768]{1,0:T(8,128)(2,1)S(1)} %get-tuple-element.35.refs_0_, s32[384,128]{1,0:T(8,128)S(1)} %get-tuple-element.36.refs_1_, s32[384,128]{1,0:T(8,128)S(1)} %get-tuple-element.37.refs_2_, bf16[776,768]{1,0:T(8,128)(2,1)S(1)} %get-tuple-element.38.refs_3_.own_ref.refs_0_, ...), custom_call_target="tpu_custom_call" | custom-call | flops 1466480000 | tf_op jit(solution)/shard_map/second/pallas_call | solution.py:213
  14.3 0.0 collective-permute-done.7.refs_7_
  14.3 1.2 %last.1 = (bf16[776,768]{1,0:T(8,128)(2,1)S(1)}, f32[384,128]{1,0:T(8,128)S(1)}) custom-call(bf16[384,768]{1,0:T(8,128)(2,1)S(1)} %get-tuple-element.35.refs_0_, s32[384,128]{1,0:T(8,128)S(1)} %get-tuple-element.36.refs_1_, s32[384,128]{1,0:T(8,128)S(1)} %get-tuple-element.37.refs_2_, bf16[776,768]{1,0:T(8,128)(2,1)S(1)} %get-tuple-element.40.refs_3_.refs_2_, ...), custom_call_target="tpu_custom_call" | custom-call | flops 1201520000 | tf_op jit(solution)/shard_map/last/pallas_call | solution.py:213
  15.5 0.7 %far_rest.1 = f32[1,384]{1,0:T(1,128)S(1)} custom-call(bf16[384,768]{1,0:T(8,128)(2,1)S(1)} %get-tuple-element.35.refs_0_, s32[384,128]{1,0:T(8,128)S(1)} %get-tuple-element.36.refs_1_, s32[384,128]{1,0:T(8,128)S(1)} %get-tuple-element.37.refs_2_, bf16[776,768]{1,0:T(8,128)(2,1)S(1)} %get-tuple-element.43.refs_3_, f32[384,128]{1,0:T(8,128)S(1)} %get-tuple-element.44.refs_4_), custom_call_target="tpu_custom_call" | custom-call | flops 848240000 | tf_op jit(solution)/shard_map/far_rest/pallas_call | solution.py:213
  16.2 1.9 %collective-permute-start.8 = (f32[1,384]{1,0:T(1,128)S(1)}, f32[1,384]{1,0:T(1,128)S(1)}, u32[]{:S(2)}, u32[]{:S(2)}) collective-permute-start(f32[1,384]{1,0:T(1,128)S(1)} %far_rest.1), channel_id=1, source_target_pairs={{0,8},{1,9},{2,10},{3,11},{4,12},{5,13},{6,14},{7,15},{8,0},{9,1},... | collective-permute-start | bytes 4616 | tf_op jit(solution)/shard_map/ppermute | solution.py:238
  18.2 2.1 %near.1 = f32[1,384]{1,0:T(1,128)S(1)} custom-call(bf16[776,768]{1,0:T(8,128)(2,1)S(1)} %get-tuple-element.38.refs_3_.own_ref.refs_0_, bf16[776,768]{1,0:T(8,128)(2,1)S(1)} %get-tuple-element.38.refs_3_.own_ref.refs_0_, bf16[776,768]{1,0:T(8,128)(2,1)S(1)} %first.1.refs_4_.refs_1_, bf16[776,768]{1,0:T(8,128)(2,1)S(1)} %get-tuple-element.40.refs_3_.refs_2_, ...), custom_call_target="tpu_custom_call" | custom-call | flops 2875000064 | tf_op jit(solution)/shard_map/near/pallas_call | solution.py:213
  20.3 0.5 %collective-permute-done.8 = f32[1,384]{1,0:T(1,128)S(1)} collective-permute-done((f32[1,384]{1,0:T(1,128)S(1)}, f32[1,384]{1,0:T(1,128)S(1)}, u32[]{:S(2)}, u32[]{:S(2)}) %collective-permute-start.8) | collective-permute-done | bytes 1568 | tf_op jit(solution)/shard_map/ppermute | solution.py:238
  20.8 0.6 %maximum_reduce_fusion = f32[384]{0:T(512)} fusion(f32[1,384]{1,0:T(1,128)S(1)} %collective-permute-done.8, f32[1,384]{1,0:T(1,128)S(1)} %near.1), kind=kLoop, calls=%fused_computation | loop fusion | flops 384 | bytes 4608 | tf_op jit(solution)/shard_map/max | solution.py:326
  (1 shorter events, 0.0 us)
Async XLA Ops:
  0.0 2.0 %collective-permute-start = (s32[384,96]{0,1:T(8,128)}, s32[384,96]{0,1:T(8,128)S(1)}, u32[]{:S(2)}, u32[]{:S(2)}) collective-permute-start(s32[384,96]{0,1:T(8,128)} %param.4), channel_id=1, source_target_pairs={{0,1},{1,0},{2,3},{3,2},{4,5},{5,4},{6,7},{7,6},{8,9},{9,8},{10,11... | collective-permute-start | bytes 442376 | tf_op jit(solution)/shard_map/ppermute | solution.py:238
  0.5 1.5 %collective-permute-start.1 = (s32[384]{0:T(512)}, s32[384]{0:T(512)S(1)}, u32[]{:S(2)}, u32[]{:S(2)}) collective-permute-start(s32[384]{0:T(512)} %refs_1_.1), channel_id=1, source_target_pairs={{0,1},{1,0},{2,3},{3,2},{4,5},{5,4},{6,7},{7,6},{8,9},{9,8},{10,11... | collective-permute-start | bytes 4616 | tf_op jit(solution)/shard_map/ppermute | solution.py:238
  0.5 1.5 %collective-permute-start.2 = (s32[384]{0:T(512)}, s32[384]{0:T(512)S(1)}, u32[]{:S(2)}, u32[]{:S(2)}) collective-permute-start(s32[384]{0:T(512)} %refs_2_.1), channel_id=1, source_target_pairs={{0,1},{1,0},{2,3},{3,2},{4,5},{5,4},{6,7},{7,6},{8,9},{9,8},{10,11... | collective-permute-start | bytes 4616 | tf_op jit(solution)/shard_map/ppermute | solution.py:238
  1.0 8.1 %copy-start = (bf16[256,768]{1,0:T(8,128)(2,1)S(1)}, bf16[256,768]{1,0:T(8,128)(2,1)}, u32[]{:S(2)}) copy-start(bf16[256,768]{1,0:T(8,128)(2,1)} %codebook_ref.1) | copy-start | bytes 1179652
  2.1 8.1 %collective-permute-start.5 = (bf16[104,768]{1,0:T(8,128)(2,1)S(1)}, bf16[104,768]{1,0:T(8,128)(2,1)S(1)}, u32[]{:S(2)}, u32[]{:S(2)}) collective-permute-start(bf16[104,768]{1,0:T(8,128)(2,1)S(1)} %join.1.packed_ref), channel_id=1, source_target_pairs={{0,2},{1,5},{2,0},{3,7},{4,6},{5,1},{6,4},{7,3},{8,10},{9,13},{10,... | collective-permute-start | bytes 479240 | tf_op jit(solution)/shard_map/ppermute | solution.py:238
  4.9 6.8 %collective-permute-start.4 = (bf16[104,384]{1,0:T(8,128)(2,1)S(1)}, bf16[104,384]{1,0:T(8,128)(2,1)S(1)}, u32[]{:S(2)}, u32[]{:S(2)}) collective-permute-start(bf16[104,384]{1,0:T(8,128)(2,1)S(1)} %pack.1.packed_ref), channel_id=1, source_target_pairs={{0,8},{1,9},{2,10},{3,11},{4,12},{5,13},{6,14},{7,15},{8,0},{9,1},... | collective-permute-start | bytes 239624 | tf_op jit(solution)/shard_map/ppermute | solution.py:238
  7.5 5.3 %collective-permute-start.3 = (bf16[104,384]{1,0:T(8,128)(2,1)S(1)}, bf16[104,384]{1,0:T(8,128)(2,1)S(1)}, u32[]{:S(2)}, u32[]{:S(2)}) collective-permute-start(bf16[104,384]{1,0:T(8,128)(2,1)S(1)} %pack.1.packed_ref), channel_id=1, source_target_pairs={{0,6},{1,7},{2,4},{3,5},{4,2},{5,3},{6,0},{7,1},{8,14},{9,15},{10,... | collective-permute-start | bytes 239624 | tf_op jit(solution)/shard_map/ppermute | solution.py:238
  10.2 2.6 %collective-permute-start.6 = (bf16[104,768]{1,0:T(8,128)(2,1)S(1)}, bf16[104,768]{1,0:T(8,128)(2,1)S(1)}, u32[]{:S(2)}, u32[]{:S(2)}) collective-permute-start(bf16[104,768]{1,0:T(8,128)(2,1)S(1)} %collective-permute-done.5.refs_0_), channel_id=1, source_target_pairs={{0,1},{1,0},{2,3},{3,2},{4,5},{5,4},{6,7},{7,6},{8,9},{9,8},{10,11... | collective-permute-start | bytes 479240 | tf_op jit(solution)/shard_map/ppermute | solution.py:238
  12.8 1.5 %collective-permute-start.7 = (bf16[104,384]{1,0:T(8,128)(2,1)S(1)}, bf16[104,384]{1,0:T(8,128)(2,1)S(1)}, u32[]{:S(2)}, u32[]{:S(2)}) collective-permute-start(bf16[104,384]{1,0:T(8,128)(2,1)S(1)} %collective-permute-done.3.refs_6_), channel_id=1, source_target_pairs={{0,1},{1,0},{2,3},{3,2},{4,5},{5,4},{6,7},{7,6},{8,9},{9,8},{10,11... | collective-permute-start | bytes 239624 | tf_op jit(solution)/shard_map/ppermute | solution.py:238
  16.2 4.5 %collective-permute-start.8 = (f32[1,384]{1,0:T(1,128)S(1)}, f32[1,384]{1,0:T(1,128)S(1)}, u32[]{:S(2)}, u32[]{:S(2)}) collective-permute-start(f32[1,384]{1,0:T(1,128)S(1)} %far_rest.1), channel_id=1, source_target_pairs={{0,8},{1,9},{2,10},{3,11},{4,12},{5,13},{6,14},{7,15},{8,0},{9,1},... | collective-permute-start | bytes 4616 | tf_op jit(solution)/shard_map/ppermute | solution.py:238

commit v6 on v5

--- a/solution.py
+++ b/solution.py
@@ -196,12 +196,12 @@
     rows, unit_refs, so_far = take(3), take(ready), take(with_so_far)
     table_refs, packed_refs, out_refs = take(min(decoded, 1)), take(decoded), take(min(decoded, 1))
     best_ref, exact_refs = refs[0], refs[1:]
+    best = score(*rows, unit_refs, so_far[0][...] if so_far else nothing((rows[0].shape[0], LANES)))
+    best_ref[...] = finish(best) if whole else best
     column0 = 0
     for packed_ref, exact_ref in zip(packed_refs, exact_refs):
         unit_kernel(packed_ref, table_refs[0], out_refs[0], exact_ref, column0)
         column0 += packed_ref.shape[1]
-    best = score(*rows, unit_refs, so_far[0][...] if so_far else nothing((rows[0].shape[0], LANES)))
-    best_ref[...] = finish(best) if whole else best
 
 
 VMEM = pl.BlockSpec(memory_space=pltpu.MemorySpace.VMEM)
@@ -271,9 +271,9 @@
         functools.partial(join_kernel, group_slots, groups), 0.3, "join", shape((packed_rows, pair_rows), bf16)
     )(packed, other_codes.T, other_cluster, other_slot)
     packed, own = lax.optimization_barrier((packed, own))
-    from_far = exchange(packed, far, far)
+    from_far = exchange(packed, far ^ 1, far ^ 1)
     arrived = [exchange(own, *pair) for pair in pairs]
-    last = exchange(packed, last_chip, last_chip)
+    last = exchange(packed, last_chip ^ 1, last_chip ^ 1)
 
     table, own_unit = call(
         own_kernel,
@@ -319,7 +319,7 @@
         rest = [more]
         units.append(more)
     _, far_best = step("far_rest", rest, [], far_best, whole=True)
-    best = exchange(far_best, far, far)
+    best = exchange(far_best, far ^ 1, far ^ 1)
     turned_scratch = [pltpu.VMEM(t.shape, t.dtype) for t in turned]
     for k in range(0, len(units), 4):
         part = call(near_kernel, 2.5, "near", row_best, turned_scratch)(own_unit, *units[k : k + 4])

time: 21.5 us -> 21.4 us (level)
  transfers between devices with their start and end apart: 9 -> 9, of which waited for: 3 -> 1; matrix products, arithmetic and copies ran while one was open for 0% -> 0% of each run, Pallas kernels for 35% -> 35%
where the time goes in v6:
time: 21.4 us; the launch traced here: 21.2 us
  starting transfers between devices  9.91 us (46%)
  Pallas kernels  9.39 us (44%)
  waiting for transfers between devices  1.19 us (6%)
  other arithmetic  0.6 us (3%)
    ppermute x9, starting transfers between devices, exchange(): return lax.ppermute(value, AXES, pairs)  9.91 us
    pallas_call x9, Pallas kernels, run(): pl.pallas_call(kernel, in_specs=[in_spec] * len(operands), out_shape=out_...  9.39 us
    ppermute x9, waiting for transfers between devices, exchange(): return lax.ppermute(value, AXES, pairs)  1.19 us
    max x1, other arithmetic, body(): best = jnp.maximum(best, part)  0.6 us
  transfers between devices with their start and end apart: 9, of which 1 were waited for; matrix products, arithmetic and copies ran while one was open for 0% of the time, Pallas kernels for 35%

profile of v6, /device:TPU:0, one launch (start us, length us, event | category | flops | bytes accessed | tf_op | source)
XLA Modules:
  0.0 21.2 jit_solution(13829280866529974241)
XLA Ops:
  0.0 0.5 %collective-permute-start = (s32[384,96]{0,1:T(8,128)}, s32[384,96]{0,1:T(8,128)S(1)}, u32[]{:S(2)}, u32[]{:S(2)}) collective-permute-start(s32[384,96]{0,1:T(8,128)} %param.4), channel_id=1, source_target_pairs={{0,1},{1,0},{2,3},{3,2},{4,5},{5,4},{6,7},{7,6},{8,9},{9,8},{10,11... | collective-permute-start | bytes 442376 | tf_op jit(solution)/shard_map/ppermute | solution.py:238
  0.5 0.1 collective-permute-start.1
  0.5 0.5 %collective-permute-start.2 = (s32[384]{0:T(512)}, s32[384]{0:T(512)S(1)}, u32[]{:S(2)}, u32[]{:S(2)}) collective-permute-start(s32[384]{0:T(512)} %refs_2_.1), channel_id=1, source_target_pairs={{0,1},{1,0},{2,3},{3,2},{4,5},{5,4},{6,7},{7,6},{8,9},{9,8},{10,11... | collective-permute-start | bytes 4616 | tf_op jit(solution)/shard_map/ppermute | solution.py:238
  1.0 0.0 copy-start
  1.0 1.0 %pack.1.packed_ref = bf16[104,384]{1,0:T(8,128)(2,1)S(1)} custom-call(s32[96,384]{1,0:T(8,128)} %bitcast.3, s32[384]{0:T(512)} %refs_1_.1, s32[384]{0:T(512)} %refs_2_.1), custom_call_target="tpu_custom_call" | custom-call | flops 345000000 | tf_op jit(solution)/shard_map/pack/pallas_call | solution.py:213
  2.0 0.0 collective-permute-done.1.cluster_ref
  2.0 0.0 collective-permute-done.2.slot_ref
  2.0 0.0 collective-permute-done
  2.1 2.9 %collective-permute-start.5 = (bf16[104,768]{1,0:T(8,128)(2,1)S(1)}, bf16[104,768]{1,0:T(8,128)(2,1)S(1)}, u32[]{:S(2)}, u32[]{:S(2)}) collective-permute-start(bf16[104,768]{1,0:T(8,128)(2,1)S(1)} %join.1.packed_ref), channel_id=1, source_target_pairs={{0,2},{1,5},{2,0},{3,7},{4,6},{5,1},{6,4},{7,3},{8,10},{9,13},{10,... | collective-permute-start | bytes 479240 | tf_op jit(solution)/shard_map/ppermute | solution.py:238
  4.9 2.2 %collective-permute-start.4 = (bf16[104,384]{1,0:T(8,128)(2,1)S(1)}, bf16[104,384]{1,0:T(8,128)(2,1)S(1)}, u32[]{:S(2)}, u32[]{:S(2)}) collective-permute-start(bf16[104,384]{1,0:T(8,128)(2,1)S(1)} %pack.1.packed_ref), channel_id=1, source_target_pairs={{0,9},{1,8},{2,11},{3,10},{4,13},{5,12},{6,15},{7,14},{8,1},{9,0},... | collective-permute-start | bytes 239624 | tf_op jit(solution)/shard_map/ppermute | solution.py:238
  7.1 1.7 %collective-permute-start.3 = (bf16[104,384]{1,0:T(8,128)(2,1)S(1)}, bf16[104,384]{1,0:T(8,128)(2,1)S(1)}, u32[]{:S(2)}, u32[]{:S(2)}) collective-permute-start(bf16[104,384]{1,0:T(8,128)(2,1)S(1)} %pack.1.packed_ref), channel_id=1, source_target_pairs={{0,7},{1,6},{2,5},{3,4},{4,3},{5,2},{6,1},{7,0},{8,15},{9,14},{10,... | collective-permute-start | bytes 239624 | tf_op jit(solution)/shard_map/ppermute | solution.py:238
  8.8 0.0 copy-done
  8.8 1.1 %decode_own.1 = (bf16[768,256]{1,0:T(8,128)(2,1)S(1)}, bf16[776,768]{1,0:T(8,128)(2,1)S(1)}) custom-call(bf16[256,768]{1,0:T(8,128)(2,1)S(1)} %copy-done, bf16[104,768]{1,0:T(8,128)(2,1)S(1)} %join.1.packed_ref), custom_call_target="tpu_custom_call" | custom-call | flops 1610000000 | tf_op jit(solution)/shard_map/decode_own/pallas_call | solution.py:213
  9.9 0.0 collective-permute-done.5.refs_0_
  9.9 0.1 collective-permute-start.6
  10.0 0.9 %first.1.refs_4_.refs_1_ = bf16[776,768]{1,0:T(8,128)(2,1)S(1)} custom-call(bf16[104,768]{1,0:T(8,128)(2,1)S(1)} %collective-permute-done.5.refs_0_, bf16[768,256]{1,0:T(8,128)(2,1)S(1)} %get-tuple-element.30.refs_1_.table_ref.refs_5_), custom_call_target="tpu_custom_call" | custom-call | flops 1059840000 | tf_op jit(solution)/shard_map/first/pallas_call | solution.py:213
  10.9 1.2 %collective-permute-done.4.packed_ref = bf16[104,384]{1,0:T(8,128)(2,1)S(1)} collective-permute-done((bf16[104,384]{1,0:T(8,128)(2,1)S(1)}, bf16[104,384]{1,0:T(8,128)(2,1)S(1)}, u32[]{:S(2)}, u32[]{:S(2)}) %collective-permute-start.4) | collective-permute-done | bytes 79904 | tf_op jit(solution)/shard_map/ppermute | solution.py:238
  12.1 0.8 %far.1 = (bf16[384,768]{1,0:T(8,128)(2,1)S(1)}, s32[384,128]{1,0:T(8,128)S(1)}, s32[384,128]{1,0:T(8,128)S(1)}) custom-call(bf16[104,384]{1,0:T(8,128)(2,1)S(1)} %collective-permute-done.4.packed_ref, bf16[768,256]{1,0:T(8,128)(2,1)S(1)} %get-tuple-element.30.refs_1_.table_ref.refs_5_), custom_call_target="tpu_custom_call" | custom-call | flops 1035000000 | tf_op jit(solution)/shard_map/far/pallas_call | solution.py:213
  12.9 0.0 collective-permute-done.3.refs_6_
  12.9 0.3 %collective-permute-start.7 = (bf16[104,384]{1,0:T(8,128)(2,1)S(1)}, bf16[104,384]{1,0:T(8,128)(2,1)S(1)}, u32[]{:S(2)}, u32[]{:S(2)}) collective-permute-start(bf16[104,384]{1,0:T(8,128)(2,1)S(1)} %collective-permute-done.3.refs_6_), channel_id=1, source_target_pairs={{0,1},{1,0},{2,3},{3,2},{4,5},{5,4},{6,7},{7,6},{8,9},{9,8},{10,11... | collective-permute-start | bytes 239624 | tf_op jit(solution)/shard_map/ppermute | solution.py:238
  13.2 0.0 collective-permute-done.6.refs_6_
  13.2 1.5 %second.1 = (bf16[776,768]{1,0:T(8,128)(2,1)S(1)}, f32[384,128]{1,0:T(8,128)S(1)}) custom-call(bf16[384,768]{1,0:T(8,128)(2,1)S(1)} %get-tuple-element.35.refs_0_, s32[384,128]{1,0:T(8,128)S(1)} %get-tuple-element.36.refs_1_, s32[384,128]{1,0:T(8,128)S(1)} %get-tuple-element.37.refs_2_, bf16[776,768]{1,0:T(8,128)(2,1)S(1)} %get-tuple-element.38.refs_3_.own_ref.refs_0_, ...), custom_call_target="tpu_custom_call" | custom-call | flops 1466480000 | tf_op jit(solution)/shard_map/second/pallas_call | solution.py:213
  14.7 0.0 collective-permute-done.7.refs_7_
  14.7 1.2 %last.1 = (bf16[776,768]{1,0:T(8,128)(2,1)S(1)}, f32[384,128]{1,0:T(8,128)S(1)}) custom-call(bf16[384,768]{1,0:T(8,128)(2,1)S(1)} %get-tuple-element.35.refs_0_, s32[384,128]{1,0:T(8,128)S(1)} %get-tuple-element.36.refs_1_, s32[384,128]{1,0:T(8,128)S(1)} %get-tuple-element.37.refs_2_, bf16[776,768]{1,0:T(8,128)(2,1)S(1)} %get-tuple-element.40.refs_3_.refs_2_, ...), custom_call_target="tpu_custom_call" | custom-call | flops 1201520000 | tf_op jit(solution)/shard_map/last/pallas_call | solution.py:213
  15.9 0.7 %far_rest.1 = f32[1,384]{1,0:T(1,128)S(1)} custom-call(bf16[384,768]{1,0:T(8,128)(2,1)S(1)} %get-tuple-element.35.refs_0_, s32[384,128]{1,0:T(8,128)S(1)} %get-tuple-element.36.refs_1_, s32[384,128]{1,0:T(8,128)S(1)} %get-tuple-element.37.refs_2_, bf16[776,768]{1,0:T(8,128)(2,1)S(1)} %get-tuple-element.43.refs_3_, f32[384,128]{1,0:T(8,128)S(1)} %get-tuple-element.44.refs_4_), custom_call_target="tpu_custom_call" | custom-call | flops 848240000 | tf_op jit(solution)/shard_map/far_rest/pallas_call | solution.py:213
  16.6 1.8 %collective-permute-start.8 = (f32[1,384]{1,0:T(1,128)S(1)}, f32[1,384]{1,0:T(1,128)S(1)}, u32[]{:S(2)}, u32[]{:S(2)}) collective-permute-start(f32[1,384]{1,0:T(1,128)S(1)} %far_rest.1), channel_id=1, source_target_pairs={{0,9},{1,8},{2,11},{3,10},{4,13},{5,12},{6,15},{7,14},{8,1},{9,0},... | collective-permute-start | bytes 4616 | tf_op jit(solution)/shard_map/ppermute | solution.py:238
  18.5 2.1 %near.1 = f32[1,384]{1,0:T(1,128)S(1)} custom-call(bf16[776,768]{1,0:T(8,128)(2,1)S(1)} %get-tuple-element.38.refs_3_.own_ref.refs_0_, bf16[776,768]{1,0:T(8,128)(2,1)S(1)} %get-tuple-element.38.refs_3_.own_ref.refs_0_, bf16[776,768]{1,0:T(8,128)(2,1)S(1)} %first.1.refs_4_.refs_1_, bf16[776,768]{1,0:T(8,128)(2,1)S(1)} %get-tuple-element.40.refs_3_.refs_2_, ...), custom_call_target="tpu_custom_call" | custom-call | flops 2875000064 | tf_op jit(solution)/shard_map/near/pallas_call | solution.py:213
  20.6 0.0 collective-permute-done.8
  20.6 0.6 %maximum_reduce_fusion = f32[384]{0:T(512)} fusion(f32[1,384]{1,0:T(1,128)S(1)} %collective-permute-done.8, f32[1,384]{1,0:T(1,128)S(1)} %near.1), kind=kLoop, calls=%fused_computation | loop fusion | flops 384 | bytes 4608 | tf_op jit(solution)/shard_map/max | solution.py:326
  (1 shorter events, 0.0 us)
Async XLA Ops:
  0.0 2.0 %collective-permute-start = (s32[384,96]{0,1:T(8,128)}, s32[384,96]{0,1:T(8,128)S(1)}, u32[]{:S(2)}, u32[]{:S(2)}) collective-permute-start(s32[384,96]{0,1:T(8,128)} %param.4), channel_id=1, source_target_pairs={{0,1},{1,0},{2,3},{3,2},{4,5},{5,4},{6,7},{7,6},{8,9},{9,8},{10,11... | collective-permute-start | bytes 442376 | tf_op jit(solution)/shard_map/ppermute | solution.py:238
  0.5 1.5 %collective-permute-start.1 = (s32[384]{0:T(512)}, s32[384]{0:T(512)S(1)}, u32[]{:S(2)}, u32[]{:S(2)}) collective-permute-start(s32[384]{0:T(512)} %refs_1_.1), channel_id=1, source_target_pairs={{0,1},{1,0},{2,3},{3,2},{4,5},{5,4},{6,7},{7,6},{8,9},{9,8},{10,11... | collective-permute-start | bytes 4616 | tf_op jit(solution)/shard_map/ppermute | solution.py:238
  0.5 1.5 %collective-permute-start.2 = (s32[384]{0:T(512)}, s32[384]{0:T(512)S(1)}, u32[]{:S(2)}, u32[]{:S(2)}) collective-permute-start(s32[384]{0:T(512)} %refs_2_.1), channel_id=1, source_target_pairs={{0,1},{1,0},{2,3},{3,2},{4,5},{5,4},{6,7},{7,6},{8,9},{9,8},{10,11... | collective-permute-start | bytes 4616 | tf_op jit(solution)/shard_map/ppermute | solution.py:238
  1.0 7.8 %copy-start = (bf16[256,768]{1,0:T(8,128)(2,1)S(1)}, bf16[256,768]{1,0:T(8,128)(2,1)}, u32[]{:S(2)}) copy-start(bf16[256,768]{1,0:T(8,128)(2,1)} %codebook_ref.1) | copy-start | bytes 1179652
  2.1 7.8 %collective-permute-start.5 = (bf16[104,768]{1,0:T(8,128)(2,1)S(1)}, bf16[104,768]{1,0:T(8,128)(2,1)S(1)}, u32[]{:S(2)}, u32[]{:S(2)}) collective-permute-start(bf16[104,768]{1,0:T(8,128)(2,1)S(1)} %join.1.packed_ref), channel_id=1, source_target_pairs={{0,2},{1,5},{2,0},{3,7},{4,6},{5,1},{6,4},{7,3},{8,10},{9,13},{10,... | collective-permute-start | bytes 479240 | tf_op jit(solution)/shard_map/ppermute | solution.py:238
  4.9 7.2 %collective-permute-start.4 = (bf16[104,384]{1,0:T(8,128)(2,1)S(1)}, bf16[104,384]{1,0:T(8,128)(2,1)S(1)}, u32[]{:S(2)}, u32[]{:S(2)}) collective-permute-start(bf16[104,384]{1,0:T(8,128)(2,1)S(1)} %pack.1.packed_ref), channel_id=1, source_target_pairs={{0,9},{1,8},{2,11},{3,10},{4,13},{5,12},{6,15},{7,14},{8,1},{9,0},... | collective-permute-start | bytes 239624 | tf_op jit(solution)/shard_map/ppermute | solution.py:238
  7.1 5.8 %collective-permute-start.3 = (bf16[104,384]{1,0:T(8,128)(2,1)S(1)}, bf16[104,384]{1,0:T(8,128)(2,1)S(1)}, u32[]{:S(2)}, u32[]{:S(2)}) collective-permute-start(bf16[104,384]{1,0:T(8,128)(2,1)S(1)} %pack.1.packed_ref), channel_id=1, source_target_pairs={{0,7},{1,6},{2,5},{3,4},{4,3},{5,2},{6,1},{7,0},{8,15},{9,14},{10,... | collective-permute-start | bytes 239624 | tf_op jit(solution)/shard_map/ppermute | solution.py:238
  9.9 3.3 %collective-permute-start.6 = (bf16[104,768]{1,0:T(8,128)(2,1)S(1)}, bf16[104,768]{1,0:T(8,128)(2,1)S(1)}, u32[]{:S(2)}, u32[]{:S(2)}) collective-permute-start(bf16[104,768]{1,0:T(8,128)(2,1)S(1)} %collective-permute-done.5.refs_0_), channel_id=1, source_target_pairs={{0,1},{1,0},{2,3},{3,2},{4,5},{5,4},{6,7},{7,6},{8,9},{9,8},{10,11... | collective-permute-start | bytes 479240 | tf_op jit(solution)/shard_map/ppermute | solution.py:238
  12.9 1.8 %collective-permute-start.7 = (bf16[104,384]{1,0:T(8,128)(2,1)S(1)}, bf16[104,384]{1,0:T(8,128)(2,1)S(1)}, u32[]{:S(2)}, u32[]{:S(2)}) collective-permute-start(bf16[104,384]{1,0:T(8,128)(2,1)S(1)} %collective-permute-done.3.refs_6_), channel_id=1, source_target_pairs={{0,1},{1,0},{2,3},{3,2},{4,5},{5,4},{6,7},{7,6},{8,9},{9,8},{10,11... | collective-permute-start | bytes 239624 | tf_op jit(solution)/shard_map/ppermute | solution.py:238
  16.6 4.0 %collective-permute-start.8 = (f32[1,384]{1,0:T(1,128)S(1)}, f32[1,384]{1,0:T(1,128)S(1)}, u32[]{:S(2)}, u32[]{:S(2)}) collective-permute-start(f32[1,384]{1,0:T(1,128)S(1)} %far_rest.1), channel_id=1, source_target_pairs={{0,9},{1,8},{2,11},{3,10},{4,13},{5,12},{6,15},{7,14},{8,1},{9,0},... | collective-permute-start | bytes 4616 | tf_op jit(solution)/shard_map/ppermute | solution.py:238
